TPU v7x, 256 devices: a whole 4x4x8 slice. The times are simulated.
256 devices in a mesh: section: 4 (over y), fsdp: 16 (over x, z_hi, core), tp: 4 (over z_lo).
Axes of the slice: x: 4, y: 4, z: 8 (z_hi: 2, z_lo: 4; z = z_hi * 4 + z_lo), core: 2. Of those that a mesh axis runs over, the one named last changes fastest.
Arguments:
- image: bfloat16 [4, 12288, 4096], P('section', 'fsdp'), may hold values from -8 to 8
- text_states: bfloat16 [4, 1152, 4096], P('section', 'fsdp', 'tp'), may hold values from -6 to 6
- caption_lengths: int32 [16, 3], P('fsdp'), may hold values from 1 to 48, 72 in all within a row
- layer_map: int32 [4], replicated, may hold values from 0 to 3, each once
- w_qkv: bfloat16 [4, 4096, 3, 2048], P('section', 'fsdp', None, 'tp'), may hold values from -0.3125 to 0.3125
- w_text_kv: bfloat16 [4, 4096, 2, 2048], P('section', 'fsdp', None, 'tp'), may hold values from -0.09375 to 0.09375
- w_out: bfloat16 [4, 2048, 4096], P('section', 'tp', 'fsdp'), may hold values from -1.1953125 to 1.1953125
Outputs:
- attended: bfloat16 [4, 12288, 4096], P('section', 'fsdp', 'tp')
Inputs may be any that keep to these rules, and one draw needn't show every extreme that they name: `caption_lengths`: each row sums to 72; every caption has at least one row. `layer_map`: a permutation of the sections.
All inputs are finite; a program needn't handle non-finite values.
Results may differ from a plain program's by a relative error of at most 0.02.
The roundings to bfloat16 on the way count: a program that leaves them out, or rounds other values in their place, can miss the bound.
Values may be sent and summed in bfloat16 or wider, within the bound.
No kernel may reach another device: no remote copies, remote signals or barrier semaphores. Data moves between devices by JAX's collectives and lax.ppermute only.
A program may use at most 128 MiB of HBM per device.

v0:
```python
import jax
import jax.numpy as jnp
from jax import lax
from jax.sharding import PartitionSpec as P

HD = 128
IMG = 256


def caption_visible(image_count, text_count, lengths):
    sample_image = jnp.arange(image_count, dtype=jnp.int32) // IMG
    boundary = jnp.cumsum(lengths)[:-1]
    positions = jnp.arange(text_count, dtype=jnp.int32)
    caption_of = jnp.sum((positions[:, None] >= boundary[None, :]).astype(jnp.int32), axis=1)
    image_seen = sample_image[:, None] == sample_image[None, :]
    text_seen = sample_image[:, None] == caption_of[None, :]
    return jnp.concatenate([image_seen, text_seen], axis=1)


def masked_attention(queries, key_image, value_image, key_text, value_text, lengths):
    keys_all = jnp.concatenate([key_image, key_text], axis=0)
    values_all = jnp.concatenate([value_image, value_text], axis=0)
    scores = jnp.einsum(
        "qhd,khd->hqk", queries, keys_all, preferred_element_type=jnp.float32
    ) * HD ** (-0.5)
    visible = caption_visible(queries.shape[0], key_text.shape[0], lengths)[None]
    highest = jnp.max(jnp.where(visible, scores, -jnp.inf), axis=-1, keepdims=True)
    raised = jnp.where(visible, jnp.exp(scores - highest), jnp.float32(0.0))
    weights = (raised / jnp.sum(raised, axis=-1, keepdims=True)).astype(jnp.bfloat16)
    mixed = jnp.einsum("hqk,khd->qhd", weights, values_all, preferred_element_type=jnp.float32)
    return mixed.astype(jnp.bfloat16).reshape(queries.shape[0], -1)


def add_product(source, shard_piece):
    return jnp.dot(source, shard_piece, preferred_element_type=jnp.float32)


def body(image, text_states, caption_lengths, layer_map, w_qkv, w_text_kv, w_out):
    image_rows = image[0]
    chosen = lax.dynamic_index_in_dim(layer_map, lax.axis_index("section"), 0, keepdims=False)
    widened = lax.all_gather(text_states, "tp", axis=2, tiled=True)
    stacked = lax.all_gather(widened, "section", axis=0, tiled=True)
    text_rows = lax.dynamic_index_in_dim(stacked, chosen, 0, keepdims=False)
    head_width = w_qkv.shape[3]
    heads_here = head_width // HD
    image_weight = w_qkv[0].reshape(w_qkv.shape[1], 3 * head_width)
    text_weight = w_text_kv[0].reshape(w_text_kv.shape[1], 2 * head_width)
    image_proj = add_product(image_rows, lax.all_gather(image_weight, "fsdp", axis=0, tiled=True))
    text_proj = add_product(text_rows, lax.all_gather(text_weight, "fsdp", axis=0, tiled=True))
    qkv = image_proj.astype(jnp.bfloat16).reshape(-1, 3, heads_here, HD)
    text_kv = text_proj.astype(jnp.bfloat16).reshape(-1, 2, heads_here, HD)
    mixed = masked_attention(
        qkv[:, 0], qkv[:, 1], qkv[:, 2], text_kv[:, 0], text_kv[:, 1], caption_lengths[0]
    )
    partial_terms = jnp.dot(
        mixed,
        lax.all_gather(w_out[0], "fsdp", axis=1, tiled=True),
        preferred_element_type=jnp.float32,
    )
    summed = lax.psum_scatter(
        partial_terms.astype(jnp.bfloat16), "tp", scatter_dimension=1, tiled=True
    )
    return summed[None]


def solution(mesh):
    return jax.shard_map(
        body,
        mesh=mesh,
        in_specs=(
            P("section", "fsdp", None),
            P("section", "fsdp", "tp"),
            P("fsdp", None),
            P(),
            P("section", "fsdp", None, "tp"),
            P("section", "fsdp", None, "tp"),
            P("section", "tp", "fsdp"),
        ),
        out_specs=P("section", "fsdp", "tp"),
        check_vma=False,
    )
```

profile of v0, /device:TPU:48, one launch (start us, length us, event | category | flops | bytes accessed | tf_op | source)
XLA Modules:
  0.0 521.0 jit_solution(2138841198908908910)
XLA Ops:
  6.5 0.0 all-gather.8.cloned.1.call-start
  6.5 18.0 %all_gather.16 = bf16[1,72,4096]{2,1,0:T(8,128)(2,1)} all-gather(bf16[1,72,1024]{2,1,0:T(8,128)(2,1)} %param.8), channel_id=1, replica_groups=mesh['section'=4,'fsdp'=16,'tp'=4] {'tp'}, dimensions={2}, use_global_device_ids=true | all-gather | bytes 737280 | tf_op jit(solution)/shard_map/all_gather | solution.py:41
  24.5 0.0 all-gather.8.cloned.1.call-update
  24.6 0.0 all-gather.10.cloned.1.call-start
  24.6 1.9 copy.36
  26.5 0.0 all-gather.10.cloned.1.call-update
  26.6 0.0 all-gather.6.cloned.1.call-start
  26.6 2.3 copy.25
  28.9 0.0 all-gather.6.cloned.1.call-update
  28.9 0.0 all-gather.12.cloned.1.call-start
  29.0 0.5 all-gather.12.cloned.1.call-update
  29.5 0.0 reduce-scatter.2.cloned.1.call-start
  29.6 1.3 dynamic_slice.8
  32.1 0.8 reduce-window.4
  33.6 0.1 fusion.27
  33.7 0.1 broadcast_compare_fusion.1
  33.8 0.4 broadcast_compare_fusion
  34.2 0.9 pad_add_fusion
  35.1 25.4 %all-gather.8.cloned.1.call-done = bf16[4,72,4096]{2,1,0:T(8,128)(2,1)} async-done(((bf16[1,72,4096]{2,1,0:T(8,128)(2,1)}), bf16[4,72,4096]{2,1,0:T(8,128)(2,1)}) %all-gather.8.cloned.1.call-update) | async-done | bytes 2359312 | tf_op jit(solution)/shard_map/all_gather | solution.py:42
  60.5 111.2 %all-gather.10.cloned.1.call-done = bf16[4096,1024]{1,0:T(8,128)(2,1)} async-done(((bf16[256,1024]{1,0:T(8,128)(2,1)}), bf16[4096,1024]{1,0:T(8,128)(2,1)}) %all-gather.10.cloned.1.call-update) | async-done | bytes 8388624 | tf_op jit(solution)/shard_map/all_gather | solution.py:49
  171.7 5.2 convolution_convert_fusion.1
  176.8 0.1 reshape.48
  176.9 0.1 fusion.37
  177.0 141.1 %all-gather.6.cloned.1.call-done = bf16[4096,1536]{0,1:T(8,128)(2,1)} async-done(((bf16[256,1536]{0,1:T(8,128)(2,1)}), bf16[4096,1536]{0,1:T(8,128)(2,1)}) %all-gather.6.cloned.1.call-update) | async-done | bytes 12582928 | tf_op jit(solution)/shard_map/all_gather | solution.py:48
  318.1 15.9 %fusion.14 = bf16[768,1536]{1,0:T(8,128)(2,1)} fusion(bf16[4096,1536]{0,1:T(8,128)(2,1)} %all-gather.6.cloned.1.call-done, bf16[1,768,4096]{2,1,0:T(8,128)(2,1)} %param.7), kind=kOutput, calls=%fused_computation.15 | convolution fusion | flops 9664856064 | bytes 21233664 | tf_op jit(solution)/shard_map/dot_general | solution.py:35
  334.0 4.1 reshape.47
  338.1 0.8 fusion.36
  339.0 0.2 copy_bitcast_fusion
  339.2 9.9 %fusion.38 = (f32[4,768]{1,0:T(4,128)S(1)}, f32[4,768,840]{1,2,0:T(8,128)}) fusion(pred[768,840]{0,1:T(8,128)(4,1)} %pad_add_fusion, bf16[768,1,4,128]{3,2,1,0:T(4,128)(2,1)S(1)} %get-tuple-element.6, bf16[72,4,128]{2,0,1:T(8,128)(2,1)S(1)} %get-tuple-element.14, bf16[768,4,128]{2,0,1:T(8,128)(2,1)S(1)} %get-tuple-element.12), kind=kOutput, calls=%fused_computation.51 | convolution fusion | flops 1340130176 | bytes 12625920 | tf_op jit(solution)/shard_map/sub | solution.py:28
  349.1 5.1 fusion.17
  354.2 39.8 %all-gather.12.cloned.1.call-done = bf16[1,512,4096]{2,1,0:T(8,128)(2,1)} async-done(((bf16[1,512,256]{2,1,0:T(8,128)(2,1)}), bf16[1,512,4096]{2,1,0:T(8,128)(2,1)}) %all-gather.12.cloned.1.call-update) | async-done | bytes 4194320 | tf_op jit(solution)/shard_map/all_gather | solution.py:57
  394.0 7.5 %convolution_convert_fusion = bf16[768,4096]{1,0:T(8,128)(2,1)} fusion(bf16[768,512]{0,1:T(8,128)(2,1)S(1)} %bitcast.50, bf16[1,512,4096]{2,1,0:T(8,128)(2,1)} %all-gather.12.cloned.1.call-done), kind=kOutput, calls=%fused_computation.6 | convolution fusion | flops 3224371200 | bytes 11272192 | tf_op jit(solution)/shard_map/dot_general | solution.py:55
  401.6 0.0 reduce-scatter.2.cloned.1.call-update
  401.6 112.9 %reduce-scatter.2.cloned.1.call-done = bf16[768,1024]{1,0:T(8,128)(2,1)} async-done(((bf16[768,4096]{1,0:T(8,128)(2,1)}), bf16[768,1024]{1,0:T(8,128)(2,1)}) %reduce-scatter.2.cloned.1.call-update) | async-done | bytes 1572880 | tf_op jit(solution)/shard_map/reduce_scatter | solution.py:60
  (3 shorter events, 0.0 us)
Async XLA Ops:
  6.5 54.0 %all-gather.8.cloned.1.call-start = ((), (), s32[]{:S(2)}) async-start(), calls=%async_computation.2 | async-start | bytes 2949120 | tf_op jit(solution)/shard_map/all_gather | solution.py:42
  24.6 147.1 %all-gather.10.cloned.1.call-start = ((), (), s32[]{:S(2)}) async-start(), calls=%async_computation.3 | async-start | bytes 8912896 | tf_op jit(solution)/shard_map/all_gather | solution.py:49
  26.6 291.5 %all-gather.6.cloned.1.call-start = ((), (), s32[]{:S(2)}) async-start(), calls=%async_computation.1 | async-start | bytes 13369344 | tf_op jit(solution)/shard_map/all_gather | solution.py:48
  28.9 365.1 %all-gather.12.cloned.1.call-start = ((), (), s32[]{:S(2)}) async-start(), calls=%async_computation.5 | async-start | bytes 4456448 | tf_op jit(solution)/shard_map/all_gather | solution.py:57
  29.5 485.0 %reduce-scatter.2.cloned.1.call-start = ((), (), s32[]{:S(2)}) async-start(), calls=%async_computation.4 | async-start | bytes 7864320 | tf_op jit(solution)/shard_map/reduce_scatter | solution.py:60
Sparse Core Ops, SparseCore 0:
  24.7 35.7 all-gather.7
  63.2 108.4 all-gather.9
  174.2 143.8 all-gather.5
  320.5 73.4 all-gather.11
  401.7 112.7 reduce-scatter.1
where the time goes:
time: 523 us; the launch traced here: 521 us
  waiting for transfers between devices  431 us (82%)
  matrix products  43.6 us (8%)
  blocking collectives  18 us (3%)
  between operations  15.1 us (3%)
  local copies, waits for them, and re-layouts  10.8 us (2%)
    all_gather x1, waiting for transfers between devices, body(): lax.all_gather(image_weight, 'fsdp', axis=0, tiled=True)  141 us
    reduce_scatter x1, waiting for transfers between devices, body(): lax.psum_scatter(partial_terms.astype(jnp.bfloat16), 'tp', scatter_dimens...  113 us
    all_gather x1, waiting for transfers between devices, body(): lax.all_gather(text_weight, 'fsdp', axis=0, tiled=True)  111 us
    all_gather x1, waiting for transfers between devices, body(): lax.all_gather(w_out[0], 'fsdp', axis=1, tiled=True)  39.8 us
    all_gather x1, waiting for transfers between devices, body(): stacked = lax.all_gather(widened, 'section', axis=0, tiled=True)  25.4 us
    dot_general x2, matrix products, add_product(): return jnp.dot(source, shard_piece, preferred_element_type=jnp.float32)  21.1 us
    all_gather x1, blocking collectives, body(): widened = lax.all_gather(text_states, 'tp', axis=2, tiled=True)  18 us
  transfers between devices with their start and end apart: 5, of which 5 were waited for; matrix products, arithmetic and copies ran while one was open for 9% of the time, Pallas kernels for 0%

commit v1 on v0

v1 whole, which is shorter than its diff:
```python
import functools

import jax
import jax.numpy as jnp
from jax import lax
from jax.experimental import pallas as pl
from jax.experimental.pallas import tpu as pltpu
from jax.sharding import PartitionSpec as P

HD = 128
IMG = 256
NX, NZ, LINE = 4, 8, 4
TROWS = 80
BF16 = jnp.bfloat16
F32 = jnp.float32
AXES = ("fsdp", "tp")


def place(x, z, core):
    return ((x * 2 + z // LINE) * 2 + core) * LINE + z % LINE


def shift(value, dx=0, dz=0, dcore=0, chosen=None):
    pairs = []
    for x in range(NX):
        for z in range(NZ):
            if chosen is not None and not chosen(x, z):
                continue
            for core in range(2):
                to = place((x + dx) % NX, (z + dz) % NZ, (core + dcore) % 2)
                pairs.append((place(x, z, core), to))
    return lax.ppermute(value, AXES, pairs)


def rotate(value, axis, step):
    return lax.ppermute(value, axis, [(i, (i + step) % 4) for i in range(4)])


def x_ring(block):
    half = block.shape[0] // 2
    from_left = shift(block, dx=1)
    from_right = shift(block, dx=-1)
    far_top = shift(from_left[:half], dx=1)
    far_bottom = shift(from_right[half:], dx=-1)
    return [block, from_left, from_right, far_top, far_bottom]


def block_parts(refs):
    out = []
    for group in range(2):
        own, left, right, top, bottom = refs[5 * group:5 * group + 5]
        half = own.shape[0] // 2
        for ref in (own, left, right):
            out += [ref.at[pl.ds(0, half)], ref.at[pl.ds(half, half)]]
        out += [top, bottom]
    return out


def head_kernel(table, columns, lengths, image_own, image_other, text_own, text_other, *rest):
    weights, (out, w, rows, text, tkv, w_sem, t_sem, i_sem) = rest[:10], rest[10:]
    depth = 256
    copies = []
    for j, part in enumerate(block_parts(weights)):
        at = pl.multiple_of(table[j] * depth, depth)
        copies.append(pltpu.make_async_copy(part, w.at[pl.ds(at, depth)], w_sem.at[j]))
    for g, source in enumerate((text_own, text_other)):
        for r in range(LINE):
            at = pl.multiple_of(columns[r] * 1024, 1024)
            copies.append(pltpu.make_async_copy(
                source.at[r], text.at[pl.ds(g * TROWS, TROWS), pl.ds(at, 1024)],
                t_sem.at[g * LINE + r]))
    for copy in copies:
        copy.start()
    for k in range(6):
        source = image_own if k < 3 else image_other
        pltpu.make_async_copy(
            source.at[pl.ds((k % 3) * IMG, IMG)], rows.at[k], i_sem.at[k]).start()
    for copy in copies:
        copy.wait()
    text_kv = jnp.dot(text[...], w[:, 3 * HD:], preferred_element_type=F32).astype(BF16)
    tkv[...] = jnp.zeros_like(tkv)
    for g in range(2):
        tkv[g, 0:TROWS, :] = text_kv[g * TROWS:(g + 1) * TROWS]

    def sample(k, carry):
        pltpu.make_async_copy(image_own.at[pl.ds(0, IMG)], rows.at[k], i_sem.at[k]).wait()
        qkv = jnp.dot(rows[k], w[:, :3 * HD], preferred_element_type=F32).astype(BF16)
        q, key, value = qkv[:, :HD], qkv[:, HD:2 * HD], qkv[:, 2 * HD:]
        g = k // 3
        j = k - 3 * g
        first = lengths[g, 0]
        second = first + lengths[g, 1]
        low = jnp.where(j == 0, 0, jnp.where(j == 1, first, second))
        high = jnp.where(j == 0, first, jnp.where(j == 1, second, 72))
        tk, tv = tkv[g, :, :HD], tkv[g, :, HD:]
        dims = (((1,), (1,)), ((), ()))
        scale = HD ** (-0.5)
        s_image = lax.dot_general(q, key, dims, preferred_element_type=F32) * scale
        s_text = lax.dot_general(q, tk, dims, preferred_element_type=F32) * scale
        position = lax.broadcasted_iota(jnp.int32, s_text.shape, 1)
        seen = (position >= low) & (position < high)
        s_text = jnp.where(seen, s_text, -jnp.inf)
        top = jnp.maximum(jnp.max(s_image, axis=1, keepdims=True),
                          jnp.max(s_text, axis=1, keepdims=True))
        e_image = jnp.exp(s_image - top)
        e_text = jnp.exp(s_text - top)
        total = (jnp.sum(e_image, axis=1, keepdims=True)
                 + jnp.sum(e_text, axis=1, keepdims=True))
        inverse = 1.0 / total
        mixed = jnp.dot((e_image * inverse).astype(BF16), value, preferred_element_type=F32)
        mixed += jnp.dot((e_text * inverse).astype(BF16), tv, preferred_element_type=F32)
        out[k] = mixed.astype(BF16)
        return carry

    lax.fori_loop(0, 6, sample, 0)


def attend(table, columns, lengths, images, texts, weights):
    smem = pl.BlockSpec(memory_space=pltpu.SMEM)
    hbm = pl.BlockSpec(memory_space=pl.ANY)
    return pl.pallas_call(
        head_kernel,
        out_shape=jax.ShapeDtypeStruct((6, IMG, HD), BF16),
        in_specs=[smem] * 3 + [hbm] * 14,
        out_specs=pl.BlockSpec(memory_space=pltpu.VMEM),
        scratch_shapes=[
            pltpu.VMEM((4096, 5 * HD), BF16),
            pltpu.VMEM((6, IMG, 4096), BF16),
            pltpu.VMEM((2 * TROWS, 4096), BF16),
            pltpu.VMEM((2, 128, 2 * HD), BF16),
            pltpu.SemaphoreType.DMA((16,)),
            pltpu.SemaphoreType.DMA((8,)),
            pltpu.SemaphoreType.DMA((6,)),
        ],
        compiler_params=pltpu.CompilerParams(vmem_limit_bytes=48 * 2**20),
        cost_estimate=pl.CostEstimate(
            flops=2 * 1536 * 4096 * 640, bytes_accessed=18 * 2**20, transcendentals=6 * 256 * 384),
    )(table, columns, lengths, *images, *texts, *weights)


def out_kernel(spots, heads, *rest):
    mixed_parts, rest = rest[:8], rest[8:]
    stacks, (out, w, m, w_sem, m_sem) = rest[:4], rest[4:]
    copies = []
    for i, stack in enumerate(stacks):
        for d in range(4):
            n = 4 * i + d
            at = pl.multiple_of(spots[n, 1] * 256, 256)
            copies.append(pltpu.make_async_copy(
                stack.at[d], w.at[spots[n, 0], :, pl.ds(at, 256)], w_sem.at[n]))
    for h in range(2):
        for r in range(LINE):
            for s in range(2):
                at = pl.multiple_of((heads[4 + s] + h) * HD, HD)
                copies.append(pltpu.make_async_copy(
                    mixed_parts[4 * h + r].at[:, pl.ds(s * HD, HD)],
                    m.at[heads[r], :, pl.ds(at, HD)], m_sem.at[(4 * h + r) * 2 + s]))
    for copy in copies:
        copy.start()
    for copy in copies:
        copy.wait()

    def tile(k, carry):
        at = pl.ds(pl.multiple_of(k * 256, 256), 256)
        total = jnp.zeros((256, 1024), F32)
        for block in range(LINE):
            term = jnp.dot(m[block, at, :], w[block], preferred_element_type=F32)
            total += term.astype(BF16).astype(F32)
        out[at, :] = total.astype(BF16)
        return carry

    lax.fori_loop(0, 3, tile, 0)


def project(spots, heads, mixed_parts, stacks):
    smem = pl.BlockSpec(memory_space=pltpu.SMEM)
    hbm = pl.BlockSpec(memory_space=pl.ANY)
    return pl.pallas_call(
        out_kernel,
        out_shape=jax.ShapeDtypeStruct((768, 1024), BF16),
        in_specs=[smem] * 2 + [hbm] * 12,
        out_specs=pl.BlockSpec(memory_space=pltpu.VMEM),
        scratch_shapes=[
            pltpu.VMEM((LINE, 512, 1024), BF16),
            pltpu.VMEM((LINE, 768, 512), BF16),
            pltpu.SemaphoreType.DMA((16,)),
            pltpu.SemaphoreType.DMA((16,)),
        ],
        compiler_params=pltpu.CompilerParams(vmem_limit_bytes=48 * 2**20),
        cost_estimate=pl.CostEstimate(
            flops=2 * 768 * 2048 * 1024, bytes_accessed=9 * 2**20, transcendentals=0),
    )(spots, heads, *mixed_parts, *stacks)


def body(image, text_states, caption_lengths, layer_map, w_qkv, w_text_kv, w_out):
    y = lax.axis_index("section")
    f = lax.axis_index("fsdp")
    t = lax.axis_index("tp")
    x, z, core = f // 4, (f // 2) % 2 * LINE + t, f % 2

    both = jnp.concatenate(
        [w_qkv[0].reshape(256, 3, 4, HD), w_text_kv[0].reshape(256, 2, 4, HD)], axis=1)

    def head_block(head):
        return lax.dynamic_index_in_dim(both, head, 2, keepdims=False).reshape(256, 5 * HD)

    gathered = []
    for h in range(2):
        swapped = shift(head_block(2 * (1 - core) + h), dcore=1)
        own = jnp.concatenate([head_block(2 * core + h), swapped], axis=0)
        gathered.append(x_ring(own) + x_ring(shift(own, dz=4)))

    chosen = lax.dynamic_index_in_dim(layer_map, y, 0, keepdims=False)
    text_here = jnp.pad(text_states[0], ((0, TROWS - 72), (0, 0)))
    options = [text_here] + [rotate(text_here, "section", -r) for r in (1, 2, 3)]
    picked = lax.select_n((chosen - y) % 4, *options)
    text_own = jnp.stack([picked] + [rotate(picked, "tp", r) for r in (1, 2, 3)])
    texts = [text_own, shift(text_own, dcore=1)]
    columns = jnp.stack([(t - r) % 4 for r in range(4)]).astype(jnp.int32)

    images = [image[0], shift(image[0], dcore=1)]
    lengths = jnp.concatenate([caption_lengths, shift(caption_lengths, dcore=1)], axis=0)

    table = []
    for group in range(2):
        for dx in (0, -1, 1, 2):
            chip = ((x + dx) % 4) * 4 + (z // LINE + group) % 2 * 2
            table += [chip + core, chip + 1 - core]
    table = jnp.stack(table).astype(jnp.int32)

    blocks = [w_out[0]] + [
        shift(w_out[0], dz=d, chosen=lambda a, b, d=d: (b + d) % NZ % LINE == a)
        for d in range(1, NZ)]
    first, last = jnp.stack(blocks[:4]), jnp.stack(blocks[4:])
    away = (x - t) % 4
    right1 = shift(first, dx=1, chosen=lambda a, b: a == b % LINE)
    left1 = shift(last, dx=-1, chosen=lambda a, b: a == b % LINE)
    right2 = shift(lax.select(away == 0, last, right1), dx=1,
                   chosen=lambda a, b: (a - b) % 4 in (0, 1))
    left2 = shift(lax.select(away == 0, first, left1), dx=-1,
                  chosen=lambda a, b: (a - b) % 4 in (0, 3))
    first = lax.select_n(away, first, right1, right2, left2)
    last = lax.select_n(away, last, right2, left2, left1)
    stacks = [first, last, shift(first, dcore=1), shift(last, dcore=1)]
    spots = []
    for other in range(2):
        for d in range(NZ):
            source = (z - d) % NZ
            spots.append(jnp.stack([source % LINE, source // LINE * 2 + (core + other) % 2]))
    spots = jnp.stack(spots).astype(jnp.int32)

    mixed_parts = []
    for h in range(2):
        mixed = attend(table, columns, lengths, images, texts, gathered[h])
        swapped = shift(mixed[3:].reshape(768, HD), dcore=1)
        mine = jnp.concatenate([mixed[:3].reshape(768, HD), swapped], axis=1)
        mixed_parts += [mine] + [rotate(mine, "tp", r) for r in (1, 2, 3)]
    heads = jnp.concatenate(
        [columns, jnp.stack([2 * core, 2 - 2 * core]).astype(jnp.int32)])
    return project(spots, heads, mixed_parts, stacks)[None]


def solution(mesh):
    return jax.shard_map(
        body,
        mesh=mesh,
        in_specs=(
            P("section", "fsdp", None),
            P("section", "fsdp", "tp"),
            P("fsdp", None),
            P(),
            P("section", "fsdp", None, "tp"),
            P("section", "fsdp", None, "tp"),
            P("section", "tp", "fsdp"),
        ),
        out_specs=P("section", "fsdp", "tp"),
        check_vma=False,
    )
```

time: 523 us -> 355 us (0.68)
  waiting for transfers between devices: 431 us -> 126 us
  starting transfers between devices: 0.17 us -> 158 us
  Pallas kernels: 0 us -> 43.8 us
  matrix products: 43.6 us -> 0 us
  blocking collectives: 18 us -> 0 us
  between operations: 15.1 us -> 1.96 us
  other arithmetic: 2.32 us -> 10.8 us
    all_gather x4 -> x0, waiting for transfers between devices: 317 us -> none  [the longest x1 141 us: body(): lax.all_gather(image_weight, 'fsdp', axis=0, tiled=True)]
    ppermute x0 -> x50, starting transfers between devices: none -> 158 us  [the longest x38 121 us: shift(): return lax.ppermute(value, AXES, pairs)]
    ppermute x0 -> x50, waiting for transfers between devices: none -> 126 us  [the longest x12 72.1 us: rotate(): return lax.ppermute(value, axis, [(i, (i + step) % 4) for i in range(4)])]
    reduce_scatter x1 -> x0, waiting for transfers between devices: 113 us -> none  [body(): lax.psum_scatter(partial_terms.astype(jnp.bfloat16), 'tp', scatter_dimens...]
    pallas_call x0 -> x3, Pallas kernels: none -> 43.8 us  [the longest x2 35.4 us: attend(): pl.pallas_call(head_kernel, out_shape=jax.ShapeDtypeStruct((6, IMG, HD),...]
    dot_general x4 -> x0, matrix products: 33.7 us -> none  [the longest x2 21.1 us: add_product(): return jnp.dot(source, shard_piece, preferred_element_type=jnp.float32)]
    all_gather x1 -> x0, blocking collectives: 18 us -> none  [body(): widened = lax.all_gather(text_states, 'tp', axis=2, tiled=True)]
    sub x1 -> x0, matrix products: 9.94 us -> none  [masked_attention(): raised = jnp.where(visible, jnp.exp(scores - highest), jnp.float32(0.0))]
  transfers between devices with their start and end apart: 5 -> 50, of which waited for: 5 -> 17; matrix products, arithmetic and copies ran while one was open for 9% -> 5% of each run, Pallas kernels for 0% -> 10%
where the time goes in v1:
time: 355 us; the launch traced here: 350 us
  starting transfers between devices  158 us (45%)
  waiting for transfers between devices  126 us (35%)
  Pallas kernels  43.8 us (12%)
  other arithmetic  10.8 us (3%)
  local copies, waits for them, and re-layouts  8.8 us (2%)
    ppermute x38, starting transfers between devices, shift(): return lax.ppermute(value, AXES, pairs)  121 us
    ppermute x12, waiting for transfers between devices, rotate(): return lax.ppermute(value, axis, [(i, (i + step) % 4) for i in range(4)])  72.1 us
    ppermute x38, waiting for transfers between devices, shift(): return lax.ppermute(value, AXES, pairs)  54.4 us
    ppermute x12, starting transfers between devices, rotate(): return lax.ppermute(value, axis, [(i, (i + step) % 4) for i in range(4)])  37.2 us
    pallas_call x2, Pallas kernels, attend(): pl.pallas_call(head_kernel, out_shape=jax.ShapeDtypeStruct((6, IMG, HD),...  35.4 us
    pallas_call x1, Pallas kernels, project(): pl.pallas_call(out_kernel, out_shape=jax.ShapeDtypeStruct((768, 1024), BF...  8.4 us
  transfers between devices with their start and end apart: 50, of which 17 were waited for; matrix products, arithmetic and copies ran while one was open for 5% of the time, Pallas kernels for 10%

profile of v1, /device:TPU:48, one launch (start us, length us, event | category | flops | bytes accessed | tf_op | source)
XLA Modules:
  0.0 350.2 jit_solution(16139931544991270620)
XLA Ops:
  0.0 2.2 collective-permute-start.44
  2.2 0.7 collective-permute-start.43
  2.9 0.7 collective-permute-start.42
  3.6 0.7 collective-permute-start.41
  4.2 15.5 %collective-permute-done.44 = bf16[512,256]{1,0:T(8,128)(2,1)S(1)} collective-permute-done((bf16[512,256]{1,0:T(8,128)(2,1)}, bf16[512,256]{1,0:T(8,128)(2,1)S(1)}, u32[]{:S(2)}, u32[]{:S(2)}) %collective-permute-start.44) | collective-permute-done | bytes 262176 | tf_op jit(solution)/shard_map/ppermute | solution.py:32
  20.5 1.1 pad_maximum_fusion.1
  21.6 1.4 collective-permute-start.46
  24.9 2.2 collective-permute-start.3
  27.0 1.1 collective-permute-done
  28.6 4.9 %collective-permute-done.3 = bf16[80,1024]{1,0:T(8,128)(2,1)S(1)} collective-permute-done((bf16[80,1024]{1,0:T(8,128)(2,1)S(1)}, bf16[80,1024]{1,0:T(8,128)(2,1)S(1)}, u32[]{:S(2)}, u32[]{:S(2)}) %collective-permute-start.3) | collective-permute-done | bytes 163872 | tf_op jit(solution)/shard_map/ppermute | solution.py:36
  33.5 17.8 %collective-permute-start.39 = (bf16[512,256]{1,0:T(8,128)(2,1)S(1)}, bf16[512,256]{1,0:T(8,128)(2,1)S(1)}, u32[]{:S(2)}, u32[]{:S(2)}) collective-permute-start(bf16[512,256]{1,0:T(8,128)(2,1)S(1)} %bitcast.126), channel_id=1, source_target_pairs={{1,8},{5,12},{9,0},{13,4},{18,25},{22,29},{26,17},{30,21},{35,42},... | collective-permute-start | bytes 786440 | tf_op jit(solution)/shard_map/ppermute | solution.py:32
  52.9 0.8 collective-permute-start.38
  53.8 3.0 collective-permute-done.2
  56.8 0.7 collective-permute-start.37
  57.6 1.0 select_select_fusion.2
  58.6 7.9 %collective-permute-start.7 = (bf16[80,1024]{1,0:T(8,128)(2,1)S(1)}, bf16[80,1024]{1,0:T(8,128)(2,1)}, u32[]{:S(2)}, u32[]{:S(2)}) collective-permute-start(bf16[80,1024]{1,0:T(8,128)(2,1)S(1)} %select_select_fusion.2), channel_id=1, source_target_pairs={{0,3},{1,0},{2,1},{3,2},{4,7},{5,4},{6,5},{7,6},{8,11},{9,8},{10,9... | collective-permute-start | bytes 491528 | tf_op jit(solution)/shard_map/ppermute | solution.py:36
  66.6 2.4 collective-permute-start.6
  68.9 0.9 copy.47
  70.1 6.0 %collective-permute-done.6 = bf16[80,1024]{1,0:T(8,128)(2,1)} collective-permute-done((bf16[80,1024]{1,0:T(8,128)(2,1)S(1)}, bf16[80,1024]{1,0:T(8,128)(2,1)}, u32[]{:S(2)}, u32[]{:S(2)}) %collective-permute-start.6) | collective-permute-done | bytes 163872 | tf_op jit(solution)/shard_map/ppermute | solution.py:36
  76.1 2.0 collective-permute-start.5
  78.1 2.7 collective-permute-start.11
  80.8 2.4 broadcast_select_fusion
  83.2 4.6 %collective-permute-start.14 = (bf16[512,640]{1,0:T(8,128)(2,1)S(1)}, bf16[512,640]{1,0:T(8,128)(2,1)S(1)}, u32[]{:S(2)}, u32[]{:S(2)}) collective-permute-start(bf16[512,640]{1,0:T(8,128)(2,1)S(1)} %pad_maximum_fusion.3.rest_0_), channel_id=1, source_target_pairs={{0,8},{4,12},{1,9},{5,13},{2,10},{6,14},{3,11},{7,15},{8,0},{12,4}... | collective-permute-start | bytes 1966088 | tf_op jit(solution)/shard_map/ppermute | solution.py:32
  87.8 0.7 collective-permute-start.40
  88.6 1.0 pad_maximum_fusion.4.rest_0_
  89.6 6.1 %collective-permute-start.24 = (bf16[512,640]{1,0:T(8,128)(2,1)S(1)}, bf16[512,640]{1,0:T(8,128)(2,1)S(1)}, u32[]{:S(2)}, u32[]{:S(2)}) collective-permute-start(bf16[512,640]{1,0:T(8,128)(2,1)S(1)} %pad_maximum_fusion.4.rest_0_), channel_id=1, source_target_pairs={{0,16},{4,20},{1,17},{5,21},{2,18},{6,22},{3,19},{7,23},{8,24},{12... | collective-permute-start | bytes 1966088 | tf_op jit(solution)/shard_map/ppermute | solution.py:32
  95.7 3.7 %collective-permute-start.28 = (bf16[512,640]{1,0:T(8,128)(2,1)S(1)}, bf16[512,640]{1,0:T(8,128)(2,1)}, u32[]{:S(2)}, u32[]{:S(2)}) collective-permute-start(bf16[512,640]{1,0:T(8,128)(2,1)S(1)} %pad_maximum_fusion.4.rest_0_), channel_id=1, source_target_pairs={{0,8},{4,12},{1,9},{5,13},{2,10},{6,14},{3,11},{7,15},{8,0},{12,4}... | collective-permute-start | bytes 1966088 | tf_op jit(solution)/shard_map/ppermute | solution.py:32
  99.5 10.7 %collective-permute-done.14.rest_5_ = bf16[512,640]{1,0:T(8,128)(2,1)S(1)} collective-permute-done((bf16[512,640]{1,0:T(8,128)(2,1)S(1)}, bf16[512,640]{1,0:T(8,128)(2,1)S(1)}, u32[]{:S(2)}, u32[]{:S(2)}) %collective-permute-start.14) | collective-permute-done | bytes 655392 | tf_op jit(solution)/shard_map/ppermute | solution.py:32
  110.2 3.6 %collective-permute-start.25 = (bf16[512,640]{1,0:T(8,128)(2,1)S(1)}, bf16[512,640]{1,0:T(8,128)(2,1)S(1)}, u32[]{:S(2)}, u32[]{:S(2)}) collective-permute-start(bf16[512,640]{1,0:T(8,128)(2,1)S(1)} %pad_maximum_fusion.4.rest_0_), channel_id=1, source_target_pairs={{0,48},{4,52},{1,49},{5,53},{2,50},{6,54},{3,51},{7,55},{8,56},{12... | collective-permute-start | bytes 1966088 | tf_op jit(solution)/shard_map/ppermute | solution.py:32
  113.8 16.1 %collective-permute-start.15 = (bf16[512,640]{1,0:T(8,128)(2,1)S(1)}, bf16[512,640]{1,0:T(8,128)(2,1)S(1)}, u32[]{:S(2)}, u32[]{:S(2)}) collective-permute-start(bf16[512,640]{1,0:T(8,128)(2,1)S(1)} %collective-permute-done.14.rest_5_), channel_id=1, source_target_pairs={{0,16},{4,20},{1,17},{5,21},{2,18},{6,22},{3,19},{7,23},{8,24},{12... | collective-permute-start | bytes 1966088 | tf_op jit(solution)/shard_map/ppermute | solution.py:32
  129.9 6.9 %collective-permute-start.16 = (bf16[512,640]{1,0:T(8,128)(2,1)S(1)}, bf16[512,640]{1,0:T(8,128)(2,1)}, u32[]{:S(2)}, u32[]{:S(2)}) collective-permute-start(bf16[512,640]{1,0:T(8,128)(2,1)S(1)} %collective-permute-done.14.rest_5_), channel_id=1, source_target_pairs={{0,48},{4,52},{1,49},{5,53},{2,50},{6,54},{3,51},{7,55},{8,56},{12... | collective-permute-start | bytes 1966088 | tf_op jit(solution)/shard_map/ppermute | solution.py:32
  137.4 1.2 broadcast_select_fusion.1
  138.6 15.5 %collective-permute-start.47 = (bf16[4,512,256]{2,1,0:T(8,128)(2,1)}, bf16[4,512,256]{2,1,0:T(8,128)(2,1)}, u32[]{:S(2)}, u32[]{:S(2)}) collective-permute-start(bf16[4,512,256]{2,1,0:T(8,128)(2,1)} %get-tuple-element.11), channel_id=1, source_target_pairs={{0,48},{4,52},{1,49},{5,53},{8,56},{12,60},{9,57},{13,61},{17,1},{... | collective-permute-start | bytes 3145736 | tf_op jit(solution)/shard_map/ppermute | solution.py:32
  154.1 1.6 collective-permute-start.45
  155.8 9.2 %collective-permute-start.30 = (bf16[512,640]{1,0:T(8,128)(2,1)}, bf16[512,640]{1,0:T(8,128)(2,1)}, u32[]{:S(2)}, u32[]{:S(2)}) collective-permute-start(bf16[512,640]{1,0:T(8,128)(2,1)} %collective-permute-done.28.rest_5_), channel_id=1, source_target_pairs={{0,48},{4,52},{1,49},{5,53},{2,50},{6,54},{3,51},{7,55},{8,56},{12... | collective-permute-start | bytes 1966088 | tf_op jit(solution)/shard_map/ppermute | solution.py:32
  164.9 1.1 pad_maximum_fusion.2.text_own
  166.1 0.9 copy-done.39
  167.4 1.1 slice.49
  168.7 1.2 slice.51
  169.9 20.8 %collective-permute-done.30.rest_7_ = bf16[512,640]{1,0:T(8,128)(2,1)} collective-permute-done((bf16[512,640]{1,0:T(8,128)(2,1)}, bf16[512,640]{1,0:T(8,128)(2,1)}, u32[]{:S(2)}, u32[]{:S(2)}) %collective-permute-start.30) | collective-permute-done | bytes 655392 | tf_op jit(solution)/shard_map/ppermute | solution.py:32
  190.8 1.0 slice.57
  191.8 3.8 %collective-permute-start.13 = (bf16[256,640]{1,0:T(8,128)(2,1)S(1)}, bf16[256,640]{1,0:T(8,128)(2,1)S(1)}, u32[]{:S(2)}, u32[]{:S(2)}) collective-permute-start(bf16[256,640]{1,0:T(8,128)(2,1)S(1)} %slice.49), channel_id=1, source_target_pairs={{0,48},{4,52},{1,49},{5,53},{2,50},{6,54},{3,51},{7,55},{8,56},{12... | collective-permute-start | bytes 983048 | tf_op jit(solution)/shard_map/ppermute | solution.py:32
  195.6 3.2 collective-permute-start.18
  198.9 2.1 select_select_fusion
  201.0 2.1 collective-permute-done.12.rest_3_
  203.1 0.7 collective-permute-done.13.rest_4_
  203.8 3.7 %collective-permute-start.27 = (bf16[256,640]{1,0:T(8,128)(2,1)S(1)}, bf16[256,640]{1,0:T(8,128)(2,1)S(1)}, u32[]{:S(2)}, u32[]{:S(2)}) collective-permute-start(bf16[256,640]{1,0:T(8,128)(2,1)S(1)} %slice.55), channel_id=1, source_target_pairs={{0,48},{4,52},{1,49},{5,53},{2,50},{6,54},{3,51},{7,55},{8,56},{12... | collective-permute-start | bytes 983048 | tf_op jit(solution)/shard_map/ppermute | solution.py:32
  207.4 2.7 collective-permute-done.17.rest_8_
  210.1 0.7 collective-permute-done.18.rest_9_
  210.8 13.1 %collective-permute-start.32 = (bf16[256,640]{1,0:T(8,128)(2,1)S(1)}, bf16[256,640]{1,0:T(8,128)(2,1)S(1)}, u32[]{:S(2)}, u32[]{:S(2)}) collective-permute-start(bf16[256,640]{1,0:T(8,128)(2,1)S(1)} %slice.57), channel_id=1, source_target_pairs={{0,48},{4,52},{1,49},{5,53},{2,50},{6,54},{3,51},{7,55},{8,56},{12... | collective-permute-start | bytes 983048 | tf_op jit(solution)/shard_map/ppermute | solution.py:32
  224.0 17.6 %shard_map.73 = bf16[6,256,128]{2,1,0:T(8,128)(2,1)S(1)} custom-call(s32[16]{0:T(128)S(1)} %stack.372.table, s32[4]{0:T(128)S(1)} %pad_add_fusion.1.columns, s32[2,3]{1,0:T(2,128)S(1)} %pad_add_fusion.lengths, bf16[768,4096]{1,0:T(8,128)(2,1)} %bitcast.144, bf16[768,4096]{1,0:T(8,128)(2,1)} %collective-permute-done.1.image_other, ...), custom_call_target="tpu_custom_call" | custom-call | flops 8053063680 | bytes 18874368 | tf_op jit(solution)/shard_map/pallas_call | solution.py:121
  242.3 17.8 %shard_map.74 = bf16[6,256,128]{2,1,0:T(8,128)(2,1)S(1)} custom-call(s32[16]{0:T(128)S(1)} %stack.372.table, s32[4]{0:T(128)S(1)} %pad_add_fusion.1.columns, s32[2,3]{1,0:T(2,128)S(1)} %pad_add_fusion.lengths, bf16[768,4096]{1,0:T(8,128)(2,1)} %bitcast.145, bf16[768,4096]{1,0:T(8,128)(2,1)} %collective-permute-done.1.image_other, ...), custom_call_target="tpu_custom_call" | custom-call | flops 8053063680 | bytes 18874368 | tf_op jit(solution)/shard_map/pallas_call | solution.py:121
  260.2 10.2 %collective-permute-start.20 = (bf16[768,256]{1,0:T(8,128)(2,1)S(1)}, bf16[768,256]{1,0:T(8,128)(2,1)S(1)}, u32[]{:S(2)}, u32[]{:S(2)}) collective-permute-start(bf16[768,256]{1,0:T(8,128)(2,1)S(1)} %pad_maximum_fusion.5.rest_0_), channel_id=1, source_target_pairs={{0,1},{1,2},{2,3},{3,0},{4,5},{5,6},{6,7},{7,4},{8,9},{9,10},{10,1... | collective-permute-start | bytes 1179656 | tf_op jit(solution)/shard_map/ppermute | solution.py:36
  270.7 3.2 collective-permute-start.21
  274.0 2.1 collective-permute-start.34
  276.1 2.9 collective-permute-start.35
  279.0 2.1 collective-permute-done.20.rest_1_
  281.1 3.9 %collective-permute-start.36 = (bf16[768,256]{1,0:T(8,128)(2,1)S(1)}, bf16[768,256]{1,0:T(8,128)(2,1)}, u32[]{:S(2)}, u32[]{:S(2)}) collective-permute-start(bf16[768,256]{1,0:T(8,128)(2,1)S(1)} %pad_maximum_fusion.6.rest_4_), channel_id=1, source_target_pairs={{0,3},{1,0},{2,1},{3,2},{4,7},{5,4},{6,5},{7,6},{8,11},{9,8},{10,9... | collective-permute-start | bytes 1179656 | tf_op jit(solution)/shard_map/ppermute | solution.py:36
  285.5 19.6 %collective-permute-done.21.rest_2_ = bf16[768,256]{1,0:T(8,128)(2,1)} collective-permute-done((bf16[768,256]{1,0:T(8,128)(2,1)S(1)}, bf16[768,256]{1,0:T(8,128)(2,1)}, u32[]{:S(2)}, u32[]{:S(2)}) %collective-permute-start.21) | collective-permute-done | bytes 393248 | tf_op jit(solution)/shard_map/ppermute | solution.py:36
  305.0 20.3 %collective-permute-done.22.rest_3_ = bf16[768,256]{1,0:T(8,128)(2,1)} collective-permute-done((bf16[768,256]{1,0:T(8,128)(2,1)S(1)}, bf16[768,256]{1,0:T(8,128)(2,1)}, u32[]{:S(2)}, u32[]{:S(2)}) %collective-permute-start.22) | collective-permute-done | bytes 393248 | tf_op jit(solution)/shard_map/ppermute | solution.py:36
  325.3 5.0 %collective-permute-done.34.rest_5_ = bf16[768,256]{1,0:T(8,128)(2,1)} collective-permute-done((bf16[768,256]{1,0:T(8,128)(2,1)S(1)}, bf16[768,256]{1,0:T(8,128)(2,1)}, u32[]{:S(2)}, u32[]{:S(2)}) %collective-permute-start.34) | collective-permute-done | bytes 393248 | tf_op jit(solution)/shard_map/ppermute | solution.py:36
  330.3 8.0 %collective-permute-done.35.rest_6_ = bf16[768,256]{1,0:T(8,128)(2,1)} collective-permute-done((bf16[768,256]{1,0:T(8,128)(2,1)S(1)}, bf16[768,256]{1,0:T(8,128)(2,1)}, u32[]{:S(2)}, u32[]{:S(2)}) %collective-permute-start.35) | collective-permute-done | bytes 393248 | tf_op jit(solution)/shard_map/ppermute | solution.py:36
  338.3 3.3 collective-permute-done.36.rest_7_
  341.6 8.4 %shard_map.75 = bf16[768,1024]{1,0:T(8,128)(2,1)} custom-call(s32[16,2]{1,0:T(8,128)S(1)} %stack.349.spots, s32[6]{0:T(128)S(1)} %concatenate.22.heads, bf16[768,256]{1,0:T(8,128)(2,1)S(1)} %pad_maximum_fusion.5.rest_0_, bf16[768,256]{1,0:T(8,128)(2,1)S(1)} %collective-permute-done.20.rest_1_, bf16[768,256]{1,0:T(8,128)(2,1)} %collective-permute-done.21.rest_2_, ...), custom_call_target="tpu_custom_call" | custom-call | flops 3221225472 | bytes 9437184 | tf_op jit(solution)/shard_map/pallas_call | solution.py:178
  (183 shorter events, 7.1 us)
Async XLA Ops:
  0.0 223.9 %collective-permute-start.1 = (bf16[768,4096]{1,0:T(8,128)(2,1)}, bf16[768,4096]{1,0:T(8,128)(2,1)}, u32[]{:S(2)}, u32[]{:S(2)}) collective-permute-start(bf16[768,4096]{1,0:T(8,128)(2,1)} %bitcast.143), channel_id=1, source_target_pairs={{0,4},{4,0},{1,5},{5,1},{2,6},{6,2},{3,7},{7,3},{8,12},{12,8},{9,1... | collective-permute-start | bytes 18874376 | tf_op jit(solution)/shard_map/ppermute | solution.py:32
  0.0 19.8 %collective-permute-start.44 = (bf16[512,256]{1,0:T(8,128)(2,1)}, bf16[512,256]{1,0:T(8,128)(2,1)S(1)}, u32[]{:S(2)}, u32[]{:S(2)}) collective-permute-start(bf16[512,256]{1,0:T(8,128)(2,1)} %bitcast.122), channel_id=1, source_target_pairs={{1,0},{5,4},{9,8},{13,12},{18,17},{22,21},{26,25},{30,29},{35,34},... | collective-permute-start | bytes 786440 | tf_op jit(solution)/shard_map/ppermute | solution.py:32
  2.2 17.6 %collective-permute-start.43 = (bf16[512,256]{1,0:T(8,128)(2,1)}, bf16[512,256]{1,0:T(8,128)(2,1)S(1)}, u32[]{:S(2)}, u32[]{:S(2)}) collective-permute-start(bf16[512,256]{1,0:T(8,128)(2,1)} %bitcast.123), channel_id=1, source_target_pairs={{2,0},{6,4},{10,8},{14,12},{19,17},{23,21},{27,25},{31,29},{32,42}... | collective-permute-start | bytes 786440 | tf_op jit(solution)/shard_map/ppermute | solution.py:32
  2.9 16.9 %collective-permute-start.42 = (bf16[512,256]{1,0:T(8,128)(2,1)}, bf16[512,256]{1,0:T(8,128)(2,1)S(1)}, u32[]{:S(2)}, u32[]{:S(2)}) collective-permute-start(bf16[512,256]{1,0:T(8,128)(2,1)} %bitcast.124), channel_id=1, source_target_pairs={{3,0},{7,4},{11,8},{15,12},{16,25},{20,29},{24,17},{28,21},{33,42}... | collective-permute-start | bytes 786440 | tf_op jit(solution)/shard_map/ppermute | solution.py:32
  3.6 16.3 %collective-permute-start.41 = (bf16[512,256]{1,0:T(8,128)(2,1)}, bf16[512,256]{1,0:T(8,128)(2,1)S(1)}, u32[]{:S(2)}, u32[]{:S(2)}) collective-permute-start(bf16[512,256]{1,0:T(8,128)(2,1)} %bitcast.125), channel_id=1, source_target_pairs={{0,8},{4,12},{8,0},{12,4},{17,25},{21,29},{25,17},{29,21},{34,42},... | collective-permute-start | bytes 786440 | tf_op jit(solution)/shard_map/ppermute | solution.py:32
  21.6 56.5 %collective-permute-start.46 = (bf16[4,512,256]{2,1,0:T(8,128)(2,1)}, bf16[4,512,256]{2,1,0:T(8,128)(2,1)}, u32[]{:S(2)}, u32[]{:S(2)}) collective-permute-start(bf16[4,512,256]{2,1,0:T(8,128)(2,1)} %pad_maximum_fusion.1), channel_id=1, source_target_pairs={{0,48},{4,52},{8,56},{12,60},{17,1},{21,5},{25,9},{29,13},{34,18},... | collective-permute-start | bytes 3145736 | tf_op jit(solution)/shard_map/ppermute | solution.py:32
  24.3 28.6 %collective-permute-start.9 = (bf16[256,640]{1,0:T(8,128)(2,1)S(1)}, bf16[256,640]{1,0:T(8,128)(2,1)S(1)}, u32[]{:S(2)}, u32[]{:S(2)}) collective-permute-start(bf16[256,640]{1,0:T(8,128)(2,1)S(1)} %copy.45), channel_id=1, source_target_pairs={{0,4},{4,0},{1,5},{5,1},{2,6},{6,2},{3,7},{7,3},{8,12},{12,8},{9,1... | collective-permute-start | bytes 983048 | tf_op jit(solution)/shard_map/ppermute | solution.py:32
  24.9 8.6 %collective-permute-start.3 = (bf16[80,1024]{1,0:T(8,128)(2,1)S(1)}, bf16[80,1024]{1,0:T(8,128)(2,1)S(1)}, u32[]{:S(2)}, u32[]{:S(2)}) collective-permute-start(bf16[80,1024]{1,0:T(8,128)(2,1)S(1)} %pad.4), channel_id=1, source_target_pairs={{0,128},{64,192},{128,0},{192,64},{1,129},{65,193},{129,1},{193,65... | collective-permute-start | bytes 491528 | tf_op jit(solution)/shard_map/ppermute | solution.py:36
  27.0 1.1 collective-permute-start
  28.1 23.1 %collective-permute-start.4 = (bf16[80,1024]{1,0:T(8,128)(2,1)S(1)}, bf16[80,1024]{1,0:T(8,128)(2,1)S(1)}, u32[]{:S(2)}, u32[]{:S(2)}) collective-permute-start(bf16[80,1024]{1,0:T(8,128)(2,1)S(1)} %pad.4), channel_id=1, source_target_pairs={{0,64},{64,128},{128,192},{192,0},{1,65},{65,129},{129,193},{193,1... | collective-permute-start | bytes 491528 | tf_op jit(solution)/shard_map/ppermute | solution.py:36
  33.5 24.0 %collective-permute-start.39 = (bf16[512,256]{1,0:T(8,128)(2,1)S(1)}, bf16[512,256]{1,0:T(8,128)(2,1)S(1)}, u32[]{:S(2)}, u32[]{:S(2)}) collective-permute-start(bf16[512,256]{1,0:T(8,128)(2,1)S(1)} %bitcast.126), channel_id=1, source_target_pairs={{1,8},{5,12},{9,0},{13,4},{18,25},{22,29},{26,17},{30,21},{35,42},... | collective-permute-start | bytes 786440 | tf_op jit(solution)/shard_map/ppermute | solution.py:32
  51.3 5.5 %collective-permute-start.2 = (bf16[80,1024]{1,0:T(8,128)(2,1)S(1)}, bf16[80,1024]{1,0:T(8,128)(2,1)}, u32[]{:S(2)}, u32[]{:S(2)}) collective-permute-start(bf16[80,1024]{1,0:T(8,128)(2,1)S(1)} %pad.4), channel_id=1, source_target_pairs={{0,192},{64,0},{128,64},{192,128},{1,193},{65,1},{129,65},{193,129... | collective-permute-start | bytes 491528 | tf_op jit(solution)/shard_map/ppermute | solution.py:36
  52.9 5.7 %collective-permute-start.38 = (bf16[512,256]{1,0:T(8,128)(2,1)S(1)}, bf16[512,256]{1,0:T(8,128)(2,1)S(1)}, u32[]{:S(2)}, u32[]{:S(2)}) collective-permute-start(bf16[512,256]{1,0:T(8,128)(2,1)S(1)} %bitcast.127), channel_id=1, source_target_pairs={{2,8},{6,12},{10,0},{14,4},{19,25},{23,29},{27,17},{31,21},{32,34}... | collective-permute-start | bytes 786440 | tf_op jit(solution)/shard_map/ppermute | solution.py:32
  56.8 9.8 %collective-permute-start.37 = (bf16[512,256]{1,0:T(8,128)(2,1)S(1)}, bf16[512,256]{1,0:T(8,128)(2,1)S(1)}, u32[]{:S(2)}, u32[]{:S(2)}) collective-permute-start(bf16[512,256]{1,0:T(8,128)(2,1)S(1)} %bitcast.128), channel_id=1, source_target_pairs={{3,8},{7,12},{11,0},{15,4},{16,17},{20,21},{24,25},{28,29},{33,34}... | collective-permute-start | bytes 786440 | tf_op jit(solution)/shard_map/ppermute | solution.py:32
  57.5 32.1 %collective-permute-start.10 = (bf16[512,640]{1,0:T(8,128)(2,1)S(1)}, bf16[512,640]{1,0:T(8,128)(2,1)S(1)}, u32[]{:S(2)}, u32[]{:S(2)}) collective-permute-start(bf16[512,640]{1,0:T(8,128)(2,1)S(1)} %pad_maximum_fusion.3.rest_0_), channel_id=1, source_target_pairs={{0,16},{4,20},{1,17},{5,21},{2,18},{6,22},{3,19},{7,23},{8,24},{12... | collective-permute-start | bytes 1966088 | tf_op jit(solution)/shard_map/ppermute | solution.py:32
  58.6 11.2 %collective-permute-start.7 = (bf16[80,1024]{1,0:T(8,128)(2,1)S(1)}, bf16[80,1024]{1,0:T(8,128)(2,1)}, u32[]{:S(2)}, u32[]{:S(2)}) collective-permute-start(bf16[80,1024]{1,0:T(8,128)(2,1)S(1)} %select_select_fusion.2), channel_id=1, source_target_pairs={{0,3},{1,0},{2,1},{3,2},{4,7},{5,4},{6,5},{7,6},{8,11},{9,8},{10,9... | collective-permute-start | bytes 491528 | tf_op jit(solution)/shard_map/ppermute | solution.py:36
  66.6 9.6 %collective-permute-start.6 = (bf16[80,1024]{1,0:T(8,128)(2,1)S(1)}, bf16[80,1024]{1,0:T(8,128)(2,1)}, u32[]{:S(2)}, u32[]{:S(2)}) collective-permute-start(bf16[80,1024]{1,0:T(8,128)(2,1)S(1)} %select_select_fusion.2), channel_id=1, source_target_pairs={{0,2},{1,3},{2,0},{3,1},{4,6},{5,7},{6,4},{7,5},{8,10},{9,11},{10,... | collective-permute-start | bytes 491528 | tf_op jit(solution)/shard_map/ppermute | solution.py:36
  69.9 18.0 %collective-permute-start.23 = (bf16[256,640]{1,0:T(8,128)(2,1)}, bf16[256,640]{1,0:T(8,128)(2,1)}, u32[]{:S(2)}, u32[]{:S(2)}) collective-permute-start(bf16[256,640]{1,0:T(8,128)(2,1)} %copy.47), channel_id=1, source_target_pairs={{0,4},{4,0},{1,5},{5,1},{2,6},{6,2},{3,7},{7,3},{8,12},{12,8},{9,1... | collective-permute-start | bytes 983048 | tf_op jit(solution)/shard_map/ppermute | solution.py:32
  76.1 7.1 %collective-permute-start.5 = (bf16[80,1024]{1,0:T(8,128)(2,1)S(1)}, bf16[80,1024]{1,0:T(8,128)(2,1)S(1)}, u32[]{:S(2)}, u32[]{:S(2)}) collective-permute-start(bf16[80,1024]{1,0:T(8,128)(2,1)S(1)} %select_select_fusion.2), channel_id=1, source_target_pairs={{0,1},{1,2},{2,3},{3,0},{4,5},{5,6},{6,7},{7,4},{8,9},{9,10},{10,1... | collective-permute-start | bytes 491528 | tf_op jit(solution)/shard_map/ppermute | solution.py:36
  78.1 17.6 %collective-permute-start.11 = (bf16[512,640]{1,0:T(8,128)(2,1)S(1)}, bf16[512,640]{1,0:T(8,128)(2,1)S(1)}, u32[]{:S(2)}, u32[]{:S(2)}) collective-permute-start(bf16[512,640]{1,0:T(8,128)(2,1)S(1)} %pad_maximum_fusion.3.rest_0_), channel_id=1, source_target_pairs={{0,48},{4,52},{1,49},{5,53},{2,50},{6,54},{3,51},{7,55},{8,56},{12... | collective-permute-start | bytes 1966088 | tf_op jit(solution)/shard_map/ppermute | solution.py:32
  83.2 54.2 %copy-start.15 = (bf16[512,256]{1,0:T(8,128)(2,1)S(1)}, bf16[512,256]{1,0:T(8,128)(2,1)}, u32[]{:S(2)}) copy-start(bf16[512,256]{1,0:T(8,128)(2,1)} %copy-done.14) | copy-start | bytes 786436
  83.2 54.2 %copy-start.18 = (bf16[512,256]{1,0:T(8,128)(2,1)S(1)}, bf16[512,256]{1,0:T(8,128)(2,1)}, u32[]{:S(2)}) copy-start(bf16[512,256]{1,0:T(8,128)(2,1)} %copy-done.17) | copy-start | bytes 786436
  83.2 54.2 %copy-start.21 = (bf16[512,256]{1,0:T(8,128)(2,1)S(1)}, bf16[512,256]{1,0:T(8,128)(2,1)}, u32[]{:S(2)}) copy-start(bf16[512,256]{1,0:T(8,128)(2,1)} %copy-done.20) | copy-start | bytes 786436
  83.2 54.2 %copy-start.24 = (bf16[512,256]{1,0:T(8,128)(2,1)S(1)}, bf16[512,256]{1,0:T(8,128)(2,1)}, u32[]{:S(2)}) copy-start(bf16[512,256]{1,0:T(8,128)(2,1)} %copy-done.23) | copy-start | bytes 786436
  83.2 26.9 %collective-permute-start.14 = (bf16[512,640]{1,0:T(8,128)(2,1)S(1)}, bf16[512,640]{1,0:T(8,128)(2,1)S(1)}, u32[]{:S(2)}, u32[]{:S(2)}) collective-permute-start(bf16[512,640]{1,0:T(8,128)(2,1)S(1)} %pad_maximum_fusion.3.rest_0_), channel_id=1, source_target_pairs={{0,8},{4,12},{1,9},{5,13},{2,10},{6,14},{3,11},{7,15},{8,0},{12,4}... | collective-permute-start | bytes 1966088 | tf_op jit(solution)/shard_map/ppermute | solution.py:32
  87.8 49.0 %collective-permute-start.40 = (bf16[4,512,256]{2,1,0:T(8,128)(2,1)S(1)}, bf16[4,512,256]{2,1,0:T(8,128)(2,1)S(1)}, u32[]{:S(2)}, u32[]{:S(2)}) collective-permute-start(bf16[4,512,256]{2,1,0:T(8,128)(2,1)S(1)} %get-tuple-element.12), channel_id=1, source_target_pairs={{0,16},{4,20},{8,24},{12,28},{17,33},{21,37},{25,41},{29,45},{34,5... | collective-permute-start | bytes 3145736 | tf_op jit(solution)/shard_map/ppermute | solution.py:32
  89.6 75.4 %copy-start.36 = (bf16[80,1024]{1,0:T(8,128)(2,1)S(1)}, bf16[80,1024]{1,0:T(8,128)(2,1)}, u32[]{:S(2)}) copy-start(bf16[80,1024]{1,0:T(8,128)(2,1)} %copy-done.35) | copy-start | bytes 491524
  89.6 77.7 %copy-start.2 = (bf16[512,640]{1,0:T(8,128)(2,1)}, bf16[512,640]{1,0:T(8,128)(2,1)S(1)}, u32[]{:S(2)}) copy-start(bf16[512,640]{1,0:T(8,128)(2,1)S(1)} %collective-permute-done.10.rest_1_) | copy-start | bytes 1966084
  89.6 24.2 %collective-permute-start.24 = (bf16[512,640]{1,0:T(8,128)(2,1)S(1)}, bf16[512,640]{1,0:T(8,128)(2,1)S(1)}, u32[]{:S(2)}, u32[]{:S(2)}) collective-permute-start(bf16[512,640]{1,0:T(8,128)(2,1)S(1)} %pad_maximum_fusion.4.rest_0_), channel_id=1, source_target_pairs={{0,16},{4,20},{1,17},{5,21},{2,18},{6,22},{3,19},{7,23},{8,24},{12... | collective-permute-start | bytes 1966088 | tf_op jit(solution)/shard_map/ppermute | solution.py:32
  95.7 70.3 %copy-start.6 = (bf16[512,640]{1,0:T(8,128)(2,1)}, bf16[512,640]{1,0:T(8,128)(2,1)S(1)}, u32[]{:S(2)}) copy-start(bf16[512,640]{1,0:T(8,128)(2,1)S(1)} %collective-permute-done.11.rest_2_) | copy-start | bytes 1966084
  95.7 34.2 %collective-permute-start.28 = (bf16[512,640]{1,0:T(8,128)(2,1)S(1)}, bf16[512,640]{1,0:T(8,128)(2,1)}, u32[]{:S(2)}, u32[]{:S(2)}) collective-permute-start(bf16[512,640]{1,0:T(8,128)(2,1)S(1)} %pad_maximum_fusion.4.rest_0_), channel_id=1, source_target_pairs={{0,8},{4,12},{1,9},{5,13},{2,10},{6,14},{3,11},{7,15},{8,0},{12,4}... | collective-permute-start | bytes 1966088 | tf_op jit(solution)/shard_map/ppermute | solution.py:32
  110.2 28.5 %collective-permute-start.25 = (bf16[512,640]{1,0:T(8,128)(2,1)S(1)}, bf16[512,640]{1,0:T(8,128)(2,1)S(1)}, u32[]{:S(2)}, u32[]{:S(2)}) collective-permute-start(bf16[512,640]{1,0:T(8,128)(2,1)S(1)} %pad_maximum_fusion.4.rest_0_), channel_id=1, source_target_pairs={{0,48},{4,52},{1,49},{5,53},{2,50},{6,54},{3,51},{7,55},{8,56},{12... | collective-permute-start | bytes 1966088 | tf_op jit(solution)/shard_map/ppermute | solution.py:32
  113.8 54.7 %copy-start.4 = (bf16[512,640]{1,0:T(8,128)(2,1)}, bf16[512,640]{1,0:T(8,128)(2,1)S(1)}, u32[]{:S(2)}) copy-start(bf16[512,640]{1,0:T(8,128)(2,1)S(1)} %collective-permute-done.24.rest_1_) | copy-start | bytes 1966084
  113.8 40.3 %collective-permute-start.15 = (bf16[512,640]{1,0:T(8,128)(2,1)S(1)}, bf16[512,640]{1,0:T(8,128)(2,1)S(1)}, u32[]{:S(2)}, u32[]{:S(2)}) collective-permute-start(bf16[512,640]{1,0:T(8,128)(2,1)S(1)} %collective-permute-done.14.rest_5_), channel_id=1, source_target_pairs={{0,16},{4,20},{1,17},{5,21},{2,18},{6,22},{3,19},{7,23},{8,24},{12... | collective-permute-start | bytes 1966088 | tf_op jit(solution)/shard_map/ppermute | solution.py:32
  129.9 25.9 %collective-permute-start.16 = (bf16[512,640]{1,0:T(8,128)(2,1)S(1)}, bf16[512,640]{1,0:T(8,128)(2,1)}, u32[]{:S(2)}, u32[]{:S(2)}) collective-permute-start(bf16[512,640]{1,0:T(8,128)(2,1)S(1)} %collective-permute-done.14.rest_5_), channel_id=1, source_target_pairs={{0,48},{4,52},{1,49},{5,53},{2,50},{6,54},{3,51},{7,55},{8,56},{12... | collective-permute-start | bytes 1966088 | tf_op jit(solution)/shard_map/ppermute | solution.py:32
  136.8 29.2 %collective-permute-start.29 = (bf16[512,640]{1,0:T(8,128)(2,1)}, bf16[512,640]{1,0:T(8,128)(2,1)S(1)}, u32[]{:S(2)}, u32[]{:S(2)}) collective-permute-start(bf16[512,640]{1,0:T(8,128)(2,1)} %collective-permute-done.28.rest_5_), channel_id=1, source_target_pairs={{0,16},{4,20},{1,17},{5,21},{2,18},{6,22},{3,19},{7,23},{8,24},{12... | collective-permute-start | bytes 1966088 | tf_op jit(solution)/shard_map/ppermute | solution.py:32
  138.6 57.0 %collective-permute-start.47 = (bf16[4,512,256]{2,1,0:T(8,128)(2,1)}, bf16[4,512,256]{2,1,0:T(8,128)(2,1)}, u32[]{:S(2)}, u32[]{:S(2)}) collective-permute-start(bf16[4,512,256]{2,1,0:T(8,128)(2,1)} %get-tuple-element.11), channel_id=1, source_target_pairs={{0,48},{4,52},{1,49},{5,53},{8,56},{12,60},{9,57},{13,61},{17,1},{... | collective-permute-start | bytes 3145736 | tf_op jit(solution)/shard_map/ppermute | solution.py:32
  154.1 41.5 %collective-permute-start.45 = (bf16[4,512,256]{2,1,0:T(8,128)(2,1)}, bf16[4,512,256]{2,1,0:T(8,128)(2,1)}, u32[]{:S(2)}, u32[]{:S(2)}) collective-permute-start(bf16[4,512,256]{2,1,0:T(8,128)(2,1)} %broadcast_select_fusion.1), channel_id=1, source_target_pairs={{0,16},{4,20},{3,19},{7,23},{8,24},{12,28},{11,27},{15,31},{16,32}... | collective-permute-start | bytes 3145736 | tf_op jit(solution)/shard_map/ppermute | solution.py:32
  155.8 35.0 %collective-permute-start.30 = (bf16[512,640]{1,0:T(8,128)(2,1)}, bf16[512,640]{1,0:T(8,128)(2,1)}, u32[]{:S(2)}, u32[]{:S(2)}) collective-permute-start(bf16[512,640]{1,0:T(8,128)(2,1)} %collective-permute-done.28.rest_5_), channel_id=1, source_target_pairs={{0,48},{4,52},{1,49},{5,53},{2,50},{6,54},{3,51},{7,55},{8,56},{12... | collective-permute-start | bytes 1966088 | tf_op jit(solution)/shard_map/ppermute | solution.py:32
  167.0 24.8 %collective-permute-start.8 = (bf16[4,80,1024]{2,1,0:T(8,128)(2,1)S(1)}, bf16[4,80,1024]{2,1,0:T(8,128)(2,1)}, u32[]{:S(2)}, u32[]{:S(2)}) collective-permute-start(bf16[4,80,1024]{2,1,0:T(8,128)(2,1)S(1)} %pad_maximum_fusion.2.text_own), channel_id=1, source_target_pairs={{0,4},{4,0},{1,5},{5,1},{2,6},{6,2},{3,7},{7,3},{8,12},{12,8},{9,1... | collective-permute-start | bytes 1966088 | tf_op jit(solution)/shard_map/ppermute | solution.py:32
  168.6 30.3 %copy-start.31 = (bf16[512,256]{1,0:T(8,128)(2,1)S(1)}, bf16[512,256]{1,0:T(8,128)(2,1)}, u32[]{:S(2)}) copy-start(bf16[512,256]{1,0:T(8,128)(2,1)} %copy-done.30) | copy-start | bytes 786436
  168.6 30.3 %copy-start.33 = (bf16[512,256]{1,0:T(8,128)(2,1)S(1)}, bf16[512,256]{1,0:T(8,128)(2,1)}, u32[]{:S(2)}) copy-start(bf16[512,256]{1,0:T(8,128)(2,1)} %copy-done.32) | copy-start | bytes 786436
  190.8 12.3 %collective-permute-start.12 = (bf16[256,640]{1,0:T(8,128)(2,1)S(1)}, bf16[256,640]{1,0:T(8,128)(2,1)S(1)}, u32[]{:S(2)}, u32[]{:S(2)}) collective-permute-start(bf16[256,640]{1,0:T(8,128)(2,1)S(1)} %slice.48), channel_id=1, source_target_pairs={{0,16},{4,20},{1,17},{5,21},{2,18},{6,22},{3,19},{7,23},{8,24},{12... | collective-permute-start | bytes 983048 | tf_op jit(solution)/shard_map/ppermute | solution.py:32
  191.8 32.1 %copy-start.1 = (bf16[4,80,1024]{2,1,0:T(8,128)(2,1)S(1)}, bf16[4,80,1024]{2,1,0:T(8,128)(2,1)}, u32[]{:S(2)}) copy-start(bf16[4,80,1024]{2,1,0:T(8,128)(2,1)} %copy-done) | copy-start | bytes 1966084
  191.8 32.1 %copy-start.3 = (bf16[512,640]{1,0:T(8,128)(2,1)S(1)}, bf16[512,640]{1,0:T(8,128)(2,1)}, u32[]{:S(2)}) copy-start(bf16[512,640]{1,0:T(8,128)(2,1)} %copy-done.2) | copy-start | bytes 1966084
  191.8 32.1 %copy-start.7 = (bf16[512,640]{1,0:T(8,128)(2,1)S(1)}, bf16[512,640]{1,0:T(8,128)(2,1)}, u32[]{:S(2)}) copy-start(bf16[512,640]{1,0:T(8,128)(2,1)} %copy-done.6) | copy-start | bytes 1966084
  191.8 32.1 %copy-start.11 = (bf16[512,640]{1,0:T(8,128)(2,1)S(1)}, bf16[512,640]{1,0:T(8,128)(2,1)}, u32[]{:S(2)}) copy-start(bf16[512,640]{1,0:T(8,128)(2,1)} %copy-done.10) | copy-start | bytes 1966084
  191.8 11.9 %collective-permute-start.13 = (bf16[256,640]{1,0:T(8,128)(2,1)S(1)}, bf16[256,640]{1,0:T(8,128)(2,1)S(1)}, u32[]{:S(2)}, u32[]{:S(2)}) collective-permute-start(bf16[256,640]{1,0:T(8,128)(2,1)S(1)} %slice.49), channel_id=1, source_target_pairs={{0,48},{4,52},{1,49},{5,53},{2,50},{6,54},{3,51},{7,55},{8,56},{12... | collective-permute-start | bytes 983048 | tf_op jit(solution)/shard_map/ppermute | solution.py:32
  195.6 14.5 %collective-permute-start.17 = (bf16[256,640]{1,0:T(8,128)(2,1)S(1)}, bf16[256,640]{1,0:T(8,128)(2,1)S(1)}, u32[]{:S(2)}, u32[]{:S(2)}) collective-permute-start(bf16[256,640]{1,0:T(8,128)(2,1)S(1)} %slice.50), channel_id=1, source_target_pairs={{0,16},{4,20},{1,17},{5,21},{2,18},{6,22},{3,19},{7,23},{8,24},{12... | collective-permute-start | bytes 983048 | tf_op jit(solution)/shard_map/ppermute | solution.py:32
  195.6 15.2 %collective-permute-start.18 = (bf16[256,640]{1,0:T(8,128)(2,1)S(1)}, bf16[256,640]{1,0:T(8,128)(2,1)S(1)}, u32[]{:S(2)}, u32[]{:S(2)}) collective-permute-start(bf16[256,640]{1,0:T(8,128)(2,1)S(1)} %slice.51), channel_id=1, source_target_pairs={{0,48},{4,52},{1,49},{5,53},{2,50},{6,54},{3,51},{7,55},{8,56},{12... | collective-permute-start | bytes 983048 | tf_op jit(solution)/shard_map/ppermute | solution.py:32
  203.1 38.6 %collective-permute-start.26 = (bf16[256,640]{1,0:T(8,128)(2,1)S(1)}, bf16[256,640]{1,0:T(8,128)(2,1)S(1)}, u32[]{:S(2)}, u32[]{:S(2)}) collective-permute-start(bf16[256,640]{1,0:T(8,128)(2,1)S(1)} %slice.54), channel_id=1, source_target_pairs={{0,16},{4,20},{1,17},{5,21},{2,18},{6,22},{3,19},{7,23},{8,24},{12... | collective-permute-start | bytes 983048 | tf_op jit(solution)/shard_map/ppermute | solution.py:32
  203.8 38.5 %collective-permute-start.27 = (bf16[256,640]{1,0:T(8,128)(2,1)S(1)}, bf16[256,640]{1,0:T(8,128)(2,1)S(1)}, u32[]{:S(2)}, u32[]{:S(2)}) collective-permute-start(bf16[256,640]{1,0:T(8,128)(2,1)S(1)} %slice.55), channel_id=1, source_target_pairs={{0,48},{4,52},{1,49},{5,53},{2,50},{6,54},{3,51},{7,55},{8,56},{12... | collective-permute-start | bytes 983048 | tf_op jit(solution)/shard_map/ppermute | solution.py:32
  210.1 32.2 %collective-permute-start.31 = (bf16[256,640]{1,0:T(8,128)(2,1)S(1)}, bf16[256,640]{1,0:T(8,128)(2,1)S(1)}, u32[]{:S(2)}, u32[]{:S(2)}) collective-permute-start(bf16[256,640]{1,0:T(8,128)(2,1)S(1)} %slice.56), channel_id=1, source_target_pairs={{0,16},{4,20},{1,17},{5,21},{2,18},{6,22},{3,19},{7,23},{8,24},{12... | collective-permute-start | bytes 983048 | tf_op jit(solution)/shard_map/ppermute | solution.py:32
  210.8 31.6 %collective-permute-start.32 = (bf16[256,640]{1,0:T(8,128)(2,1)S(1)}, bf16[256,640]{1,0:T(8,128)(2,1)S(1)}, u32[]{:S(2)}, u32[]{:S(2)}) collective-permute-start(bf16[256,640]{1,0:T(8,128)(2,1)S(1)} %slice.57), channel_id=1, source_target_pairs={{0,48},{4,52},{1,49},{5,53},{2,50},{6,54},{3,51},{7,55},{8,56},{12... | collective-permute-start | bytes 983048 | tf_op jit(solution)/shard_map/ppermute | solution.py:32
  223.9 50.1 %collective-permute-start.48 = (bf16[4,512,256]{2,1,0:T(8,128)(2,1)S(1)}, bf16[4,512,256]{2,1,0:T(8,128)(2,1)S(1)}, u32[]{:S(2)}, u32[]{:S(2)}) collective-permute-start(bf16[4,512,256]{2,1,0:T(8,128)(2,1)S(1)} %get-tuple-element.6.rest_8_), channel_id=1, source_target_pairs={{0,4},{4,0},{1,5},{5,1},{2,6},{6,2},{3,7},{7,3},{8,12},{12,8},{9,1... | collective-permute-start | bytes 3145736 | tf_op jit(solution)/shard_map/ppermute | solution.py:32
  241.7 34.5 %collective-permute-start.49 = (bf16[4,512,256]{2,1,0:T(8,128)(2,1)S(1)}, bf16[4,512,256]{2,1,0:T(8,128)(2,1)S(1)}, u32[]{:S(2)}, u32[]{:S(2)}) collective-permute-start(bf16[4,512,256]{2,1,0:T(8,128)(2,1)S(1)} %get-tuple-element.5.rest_9_), channel_id=1, source_target_pairs={{0,4},{4,0},{1,5},{5,1},{2,6},{6,2},{3,7},{7,3},{8,12},{12,8},{9,1... | collective-permute-start | bytes 3145736 | tf_op jit(solution)/shard_map/ppermute | solution.py:32
  242.2 17.9 %collective-permute-start.19 = (bf16[768,128]{1,0:T(8,128)(2,1)S(1)}, bf16[768,128]{1,0:T(8,128)(2,1)S(1)}, u32[]{:S(2)}, u32[]{:S(2)}) collective-permute-start(bf16[768,128]{1,0:T(8,128)(2,1)S(1)} %bitcast.140), channel_id=1, source_target_pairs={{0,4},{4,0},{1,5},{5,1},{2,6},{6,2},{3,7},{7,3},{8,12},{12,8},{9,1... | collective-permute-start | bytes 589832 | tf_op jit(solution)/shard_map/ppermute | solution.py:32
  260.2 20.9 %collective-permute-start.20 = (bf16[768,256]{1,0:T(8,128)(2,1)S(1)}, bf16[768,256]{1,0:T(8,128)(2,1)S(1)}, u32[]{:S(2)}, u32[]{:S(2)}) collective-permute-start(bf16[768,256]{1,0:T(8,128)(2,1)S(1)} %pad_maximum_fusion.5.rest_0_), channel_id=1, source_target_pairs={{0,1},{1,2},{2,3},{3,0},{4,5},{5,6},{6,7},{7,4},{8,9},{9,10},{10,1... | collective-permute-start | bytes 1179656 | tf_op jit(solution)/shard_map/ppermute | solution.py:36
  270.4 3.6 %collective-permute-start.33 = (bf16[768,128]{1,0:T(8,128)(2,1)S(1)}, bf16[768,128]{1,0:T(8,128)(2,1)S(1)}, u32[]{:S(2)}, u32[]{:S(2)}) collective-permute-start(bf16[768,128]{1,0:T(8,128)(2,1)S(1)} %bitcast.141), channel_id=1, source_target_pairs={{0,4},{4,0},{1,5},{5,1},{2,6},{6,2},{3,7},{7,3},{8,12},{12,8},{9,1... | collective-permute-start | bytes 589832 | tf_op jit(solution)/shard_map/ppermute | solution.py:32
  270.7 34.3 %collective-permute-start.21 = (bf16[768,256]{1,0:T(8,128)(2,1)S(1)}, bf16[768,256]{1,0:T(8,128)(2,1)}, u32[]{:S(2)}, u32[]{:S(2)}) collective-permute-start(bf16[768,256]{1,0:T(8,128)(2,1)S(1)} %pad_maximum_fusion.5.rest_0_), channel_id=1, source_target_pairs={{0,2},{1,3},{2,0},{3,1},{4,6},{5,7},{6,4},{7,5},{8,10},{9,11},{10,... | collective-permute-start | bytes 1179656 | tf_op jit(solution)/shard_map/ppermute | solution.py:36
  273.9 51.4 %collective-permute-start.22 = (bf16[768,256]{1,0:T(8,128)(2,1)S(1)}, bf16[768,256]{1,0:T(8,128)(2,1)}, u32[]{:S(2)}, u32[]{:S(2)}) collective-permute-start(bf16[768,256]{1,0:T(8,128)(2,1)S(1)} %pad_maximum_fusion.5.rest_0_), channel_id=1, source_target_pairs={{0,3},{1,0},{2,1},{3,2},{4,7},{5,4},{6,5},{7,6},{8,11},{9,8},{10,9... | collective-permute-start | bytes 1179656 | tf_op jit(solution)/shard_map/ppermute | solution.py:36
  274.0 56.3 %collective-permute-start.34 = (bf16[768,256]{1,0:T(8,128)(2,1)S(1)}, bf16[768,256]{1,0:T(8,128)(2,1)}, u32[]{:S(2)}, u32[]{:S(2)}) collective-permute-start(bf16[768,256]{1,0:T(8,128)(2,1)S(1)} %pad_maximum_fusion.6.rest_4_), channel_id=1, source_target_pairs={{0,1},{1,2},{2,3},{3,0},{4,5},{5,6},{6,7},{7,4},{8,9},{9,10},{10,1... | collective-permute-start | bytes 1179656 | tf_op jit(solution)/shard_map/ppermute | solution.py:36
  276.1 62.2 %collective-permute-start.35 = (bf16[768,256]{1,0:T(8,128)(2,1)S(1)}, bf16[768,256]{1,0:T(8,128)(2,1)}, u32[]{:S(2)}, u32[]{:S(2)}) collective-permute-start(bf16[768,256]{1,0:T(8,128)(2,1)S(1)} %pad_maximum_fusion.6.rest_4_), channel_id=1, source_target_pairs={{0,2},{1,3},{2,0},{3,1},{4,6},{5,7},{6,4},{7,5},{8,10},{9,11},{10,... | collective-permute-start | bytes 1179656 | tf_op jit(solution)/shard_map/ppermute | solution.py:36
  281.1 60.5 %collective-permute-start.36 = (bf16[768,256]{1,0:T(8,128)(2,1)S(1)}, bf16[768,256]{1,0:T(8,128)(2,1)}, u32[]{:S(2)}, u32[]{:S(2)}) collective-permute-start(bf16[768,256]{1,0:T(8,128)(2,1)S(1)} %pad_maximum_fusion.6.rest_4_), channel_id=1, source_target_pairs={{0,3},{1,0},{2,1},{3,2},{4,7},{5,4},{6,5},{7,6},{8,11},{9,8},{10,9... | collective-permute-start | bytes 1179656 | tf_op jit(solution)/shard_map/ppermute | solution.py:36
  (37 other events, 550.0 us)

commit v2 on v1

v2 whole, which is shorter than its diff:
```python
import functools

import jax
import jax.numpy as jnp
from jax import lax
from jax.experimental import pallas as pl
from jax.experimental.pallas import tpu as pltpu
from jax.sharding import PartitionSpec as P

HD = 128
IMG = 256
NX, NZ, LINE = 4, 8, 4
LOG2E = 1.4426950408889634
TROWS = 80
BF16 = jnp.bfloat16
F32 = jnp.float32
AXES = ("fsdp", "tp")


def place(x, z, core):
    return ((x * 2 + z // LINE) * 2 + core) * LINE + z % LINE


def shift(value, dx=0, dz=0, dcore=0):
    pairs = []
    for x in range(NX):
        for z in range(NZ):
            for core in range(2):
                to = place((x + dx) % NX, (z + dz) % NZ, (core + dcore) % 2)
                pairs.append((place(x, z, core), to))
    return lax.ppermute(value, AXES, pairs)


def rotate(value, axis, step):
    return lax.ppermute(value, axis, [(i, (i + step) % 4) for i in range(4)])


def after(value, *others):
    return lax.optimization_barrier((value, *others))[0] if others else value


def transposed(value, dz=0):
    pairs = []
    for x in range(NX):
        for z in range(NZ):
            for core in range(2):
                to = place(z % LINE, (z // LINE * LINE + x + dz) % NZ, core)
                pairs.append((place(x, z, core), to))
    return lax.ppermute(value, AXES, pairs)


def x_all(block, *gate):
    block = after(block, *gate)
    return [block] + [shift(block, dx=d) for d in (1, -1, 2)]


def x_gather(block):
    return lax.all_gather(
        block, "fsdp", axis_index_groups=[[4 * x + rest for x in range(NX)] for rest in range(4)])


def block_parts(refs, depth):
    out = []
    for ref in refs:
        for view in [ref] if len(ref.shape) == 2 else [ref.at[i] for i in range(ref.shape[0])]:
            out += [view.at[pl.ds(i * depth, depth)] for i in range(view.shape[0] // depth)]
    return out


def text_kernel(table, text_own, text_other, from_low, from_high, *rest):
    outs, (w, text, w_sem, t_sem) = rest[:4], rest[4:]
    copies = []
    for j, part in enumerate(block_parts((from_low, from_high), 256)):
        at = pl.multiple_of(table[j] * 256, 256)
        copies.append(pltpu.make_async_copy(part, w.at[pl.ds(at, 256)], w_sem.at[j]))
    for g, source in enumerate((text_own, text_other)):
        for r in range(4):
            copies.append(pltpu.make_async_copy(
                source.at[-r % 4], text.at[r, pl.ds(g * TROWS, TROWS)], t_sem.at[4 * g + r]))
    for copy in copies:
        copy.start()
    for copy in copies:
        copy.wait()
    for r in range(4):
        outs[r][...] = jnp.dot(
            text[r], w[...], preferred_element_type=F32).astype(outs[r].dtype)


def project_text(table, texts, weights):
    smem = pl.BlockSpec(memory_space=pltpu.SMEM)
    hbm = pl.BlockSpec(memory_space=pl.ANY)
    return pl.pallas_call(
        text_kernel,
        out_shape=[jax.ShapeDtypeStruct((2 * TROWS, 4 * HD), F32 if r == 0 else BF16)
                   for r in range(4)],
        in_specs=[smem] + [hbm] * 4,
        out_specs=[pl.BlockSpec(memory_space=pltpu.VMEM)] * 4,
        scratch_shapes=[
            pltpu.VMEM((1024, 4 * HD), BF16),
            pltpu.VMEM((4, 2 * TROWS, 1024), BF16),
            pltpu.SemaphoreType.DMA((4,)),
            pltpu.SemaphoreType.DMA((8,)),
        ],
        compiler_params=pltpu.CompilerParams(vmem_limit_bytes=24 * 2**20),
        cost_estimate=pl.CostEstimate(
            flops=2 * 640 * 1024 * 512, bytes_accessed=4 * 2**20, transcendentals=0),
    )(table, *texts, *weights)


def head_kernel(side, table, lengths, image_own, image_other, *rest):
    parts, weights = rest[:4], rest[4:-10]
    out, w, rows, text, sent, tkv, qkv, w_sem, t_sem, i_sem = rest[-10:]
    depth = 256
    copies = []
    for j, part in enumerate(block_parts(weights, depth)):
        at = pl.multiple_of(table[j] * depth, depth)
        copies.append(pltpu.make_async_copy(part, w.at[pl.ds(at, depth)], w_sem.at[j]))
    for r in range(4):
        copies.append(pltpu.make_async_copy(
            parts[r].at[:, pl.ds(side * 2 * HD, 2 * HD)], text if r == 0 else sent.at[r - 1],
            t_sem.at[r]))
    for copy in copies:
        copy.start()
    for k in range(6):
        source = image_own if k < 3 else image_other
        pltpu.make_async_copy(
            source.at[pl.ds((k % 3) * IMG, IMG)],
            rows.at[k // 3, pl.ds((k % 3) * IMG, IMG)], i_sem.at[k]).start()
    for copy in copies:
        copy.wait()
    text_kv = (text[...] + sent[0].astype(F32) + sent[1].astype(F32)
               + sent[2].astype(F32)).astype(BF16)
    tkv[...] = jnp.zeros_like(tkv)
    for g in range(2):
        tkv[g, 0:TROWS, :] = text_kv[g * TROWS:(g + 1) * TROWS]

    def load(k):
        g = k // 3
        here = pl.ds(pl.multiple_of((k - 3 * g) * IMG, IMG), IMG)
        pltpu.make_async_copy(
            image_own.at[pl.ds(0, IMG)], rows.at[g, here], i_sem.at[k]).wait()

    def compute(k):
        g = k // 3
        here = pl.ds(pl.multiple_of((k - 3 * g) * IMG, IMG), IMG)
        qkv[k % 2] = jnp.dot(rows[g, here], w[...], preferred_element_type=F32).astype(BF16)

    def mix(k):
        g = k // 3
        j = k - 3 * g
        q, key, value = qkv[k % 2, :, :HD], qkv[k % 2, :, HD:2 * HD], qkv[k % 2, :, 2 * HD:]
        first = lengths[g, 0]
        second = first + lengths[g, 1]
        low = jnp.where(j == 0, 0, jnp.where(j == 1, first, second))
        high = jnp.where(j == 0, first, jnp.where(j == 1, second, 72))
        tk, tv = tkv[g, :, :HD], tkv[g, :, HD:]
        dims = (((1,), (1,)), ((), ()))
        scale = HD ** (-0.5) * LOG2E
        s_image = lax.dot_general(q, key, dims, preferred_element_type=F32) * scale
        s_text = lax.dot_general(q, tk, dims, preferred_element_type=F32) * scale
        position = lax.broadcasted_iota(jnp.int32, s_text.shape, 1)
        seen = (position >= low) & (position < high)
        s_text = jnp.where(seen, s_text, -jnp.inf)
        top = jnp.maximum(jnp.max(s_image, axis=1, keepdims=True),
                          jnp.max(s_text, axis=1, keepdims=True))
        e_image = jnp.exp2(s_image - top)
        e_text = jnp.exp2(s_text - top)
        total = (jnp.sum(e_image, axis=1, keepdims=True)
                 + jnp.sum(e_text, axis=1, keepdims=True))
        inverse = 1.0 / total
        mixed = jnp.dot((e_image * inverse).astype(BF16), value, preferred_element_type=F32)
        mixed += jnp.dot((e_text * inverse).astype(BF16), tv, preferred_element_type=F32)
        out[k] = mixed.astype(BF16)

    load(0)
    compute(0)

    def step(k, carry):
        load(k + 1)
        compute(k + 1)
        mix(k)
        return carry

    lax.fori_loop(0, 5, step, 0)
    mix(5)


def attend(side, table, lengths, images, parts, weights):
    smem = pl.BlockSpec(memory_space=pltpu.SMEM)
    hbm = pl.BlockSpec(memory_space=pl.ANY)
    return pl.pallas_call(
        functools.partial(head_kernel, side),
        out_shape=jax.ShapeDtypeStruct((6, IMG, HD), BF16),
        in_specs=[smem] * 2 + [hbm] * (6 + len(weights)),
        out_specs=pl.BlockSpec(memory_space=pltpu.VMEM),
        scratch_shapes=[
            pltpu.VMEM((4096, 3 * HD), BF16),
            pltpu.VMEM((2, 3 * IMG, 4096), BF16),
            pltpu.VMEM((2 * TROWS, 2 * HD), F32),
            pltpu.VMEM((3, 2 * TROWS, 2 * HD), BF16),
            pltpu.VMEM((2, 128, 2 * HD), BF16),
            pltpu.VMEM((2, IMG, 3 * HD), BF16),
            pltpu.SemaphoreType.DMA((16,)),
            pltpu.SemaphoreType.DMA((4,)),
            pltpu.SemaphoreType.DMA((6,)),
        ],
        compiler_params=pltpu.CompilerParams(vmem_limit_bytes=48 * 2**20),
        cost_estimate=pl.CostEstimate(
            flops=2 * 1536 * 4096 * 512, bytes_accessed=16 * 2**20, transcendentals=6 * 256 * 384),
    )(table, lengths, *images, *parts, *weights)


def out_kernel(spots, heads, *rest):
    mixed_parts, rest = rest[:2], rest[2:]
    stacks, (out, w, m, total, w_sem, m_sem) = rest[:2], rest[2:]
    w_copies, m_copies = [], []
    for n, part in enumerate(block_parts(stacks, 512)):
        at = pl.multiple_of(spots[n, 1] * 256, 256)
        w_copies.append(pltpu.make_async_copy(
            part, w.at[spots[n, 0], :, pl.ds(at, 256)], w_sem.at[n]))
    for r in range(LINE):
        for h in range(2):
            for s in range(2):
                at = pl.multiple_of((heads[s] + h) * HD, HD)
                m_copies.append(pltpu.make_async_copy(
                    mixed_parts[h].at[r, :, pl.ds(s * HD, HD)],
                    m.at[r, :, pl.ds(at, HD)], m_sem.at[4 * r + 2 * h + s]))
    for copy in w_copies + m_copies:
        copy.start()
    for copy in w_copies:
        copy.wait()
    for r in range(LINE):
        for copy in m_copies[4 * r:4 * r + 4]:
            copy.wait()
        for k in range(3):
            at = slice(256 * k, 256 * k + 256)
            term = jnp.dot(m[r, at, :], w[(r + 2) % LINE], preferred_element_type=F32)
            term = term.astype(BF16).astype(F32)
            if r == 0:
                total[at, :] = term
            elif r < LINE - 1:
                total[at, :] += term
            else:
                out[at, :] = (total[at, :] + term).astype(BF16)


def project(spots, heads, mixed_parts, stacks):
    smem = pl.BlockSpec(memory_space=pltpu.SMEM)
    hbm = pl.BlockSpec(memory_space=pl.ANY)
    return pl.pallas_call(
        out_kernel,
        out_shape=jax.ShapeDtypeStruct((768, 1024), BF16),
        in_specs=[smem] * 2 + [hbm] * 4,
        out_specs=pl.BlockSpec(memory_space=pltpu.VMEM),
        scratch_shapes=[
            pltpu.VMEM((LINE, 512, 1024), BF16),
            pltpu.VMEM((LINE, 768, 512), BF16),
            pltpu.VMEM((768, 1024), F32),
            pltpu.SemaphoreType.DMA((16,)),
            pltpu.SemaphoreType.DMA((16,)),
        ],
        compiler_params=pltpu.CompilerParams(vmem_limit_bytes=48 * 2**20),
        cost_estimate=pl.CostEstimate(
            flops=2 * 768 * 2048 * 1024, bytes_accessed=9 * 2**20, transcendentals=0),
    )(spots, heads, *mixed_parts, *stacks)


def body(image, text_states, caption_lengths, layer_map, w_qkv, w_text_kv, w_out):
    y = lax.axis_index("section")
    f = lax.axis_index("fsdp")
    t = lax.axis_index("tp")
    x, z, core = f // 4, (f // 2) % 2 * LINE + t, f % 2

    image_weight = w_qkv[0].reshape(256, 3, 4, HD)
    text_weight = w_text_kv[0].reshape(256, 2, 4, HD)

    def head_columns(side):
        heads = [2 * side, 2 * side + 1]
        return jnp.concatenate(
            [image_weight[:, i, n] for n in heads for i in range(3)]
            + [text_weight[:, i, n] for n in heads for i in range(2)], axis=1)

    side0, side1 = head_columns(0), head_columns(1)
    sent = jnp.concatenate(
        [lax.select(core == 0, side1, side0),
         jnp.pad(caption_lengths.astype(BF16), ((0, 15), (0, 10 * HD - 3)))])
    got = shift(sent, dcore=1)
    lengths = jnp.concatenate([caption_lengths, got[256:257, :3].astype(jnp.int32)])
    both = jnp.concatenate([lax.select(core == 0, side0, side1), got[:256]])
    cuts = [both[:, :3 * HD], both[:, 3 * HD:6 * HD], both[:, 6 * HD:]]

    chosen = lax.dynamic_index_in_dim(layer_map, y, 0, keepdims=False)
    text_here = jnp.pad(text_states[0], ((0, TROWS - 72), (0, 0)))
    options = [text_here] + [rotate(text_here, "section", -r) for r in (1, 2, 3)]
    picked = lax.select_n((chosen - y) % 4, *options)

    def z_pair(block, *gate):
        block = after(block, *gate)
        return [shift(block, dz=2), shift(block, dz=-2)]

    wide = jnp.stack([picked] + [rotate(picked, "tp", r) for r in (1, 2, 3)])
    pair0 = z_pair(cuts[0], got, picked)

    weights0 = x_gather(jnp.concatenate(pair0))
    slices = [lax.dynamic_index_in_dim(wide, (t - x - d) % 4, 0, keepdims=False) for d in range(4)]
    text_own = jnp.stack(slices[:1] + [shift(slices[d], dx=d) for d in (1, 2, 3)])
    pair_text = z_pair(cuts[2], wide, *pair0)
    images = [image[0], shift(after(image[0], wide, got), dcore=1)]

    texts = [text_own, shift(after(text_own, *pair_text), dcore=1)]

    def rows_at(source, dz):
        chip = source % 4 * 4 + (z + dz) % NZ // LINE * 2
        return [chip + core, chip + 1 - core]

    def table_of(sources):
        rows = [row for source in sources for dz in (-2, 2) for row in rows_at(source, dz)]
        return jnp.stack(rows).astype(jnp.int32)

    text_parts = list(project_text(table_of([x]) % 4, texts, pair_text))
    text_parts = text_parts[:1] + [shift(text_parts[r], dx=r) for r in (1, 2, 3)]
    pair1 = z_pair(cuts[1], texts[1])

    weights1 = x_gather(jnp.concatenate(pair1))
    w_out_here = after(w_out[0], *text_parts[1:])
    pieces = jnp.concatenate([transposed(w_out_here), transposed(w_out_here, dz=4)])
    mixed0 = attend(
        0, table_of(range(NX)), lengths, images,
        [text_parts[0], *after(tuple(text_parts[1:]), *pair1)], [weights0])

    def swap_rows(mixed):
        swapped = shift(mixed[3:].reshape(768, HD), dcore=1)
        return jnp.concatenate([mixed[:3].reshape(768, HD), swapped], axis=1)

    mine0 = swap_rows(mixed0)
    mixed1 = attend(
        1, after(table_of(range(NX)), mine0, pieces), lengths, images, text_parts, [weights1])

    mine1 = swap_rows(mixed1)
    mixed_parts = [lax.all_gather(mine0, "tp"), lax.all_gather(mine1, "tp")]
    stack = jnp.concatenate(x_all(pieces, mine1))
    stacks = [stack, shift(stack, dcore=1)]
    spots = []
    for other in range(2):
        for dx in (0, -1, 1, 2):
            for dz in (0, 4):
                spots.append(jnp.stack(
                    [(x + dx) % 4, (z + dz) % NZ // LINE * 2 + (core + other) % 2]))
    spots = jnp.stack(spots).astype(jnp.int32)
    heads = jnp.stack([2 * core, 2 - 2 * core]).astype(jnp.int32)
    return project(spots, heads, mixed_parts, stacks)[None]


def solution(mesh):
    return jax.shard_map(
        body,
        mesh=mesh,
        in_specs=(
            P("section", "fsdp", None),
            P("section", "fsdp", "tp"),
            P("fsdp", None),
            P(),
            P("section", "fsdp", None, "tp"),
            P("section", "fsdp", None, "tp"),
            P("section", "tp", "fsdp"),
        ),
        out_specs=P("section", "fsdp", "tp"),
        check_vma=False,
    )
```

time: 355 us -> 281 us (0.79)
  starting transfers between devices: 158 us -> 51 us
  waiting for transfers between devices: 126 us -> 144 us
  between operations: 1.96 us -> 14.9 us
  local copies, waits for them, and re-layouts: 8.8 us -> 16.3 us
  other arithmetic: 10.8 us -> 6.17 us
    ppermute x38 -> x21, starting transfers between devices: 121 us -> 32.7 us  [shift(): return lax.ppermute(value, AXES, pairs)]
    ppermute x12 -> x6, waiting for transfers between devices: 72.1 us -> 15.4 us  [rotate(): return lax.ppermute(value, axis, [(i, (i + step) % 4) for i in range(4)])]
    ppermute x0 -> x2, waiting for transfers between devices: none -> 29.4 us  [transposed(): return lax.ppermute(value, AXES, pairs)]
    ppermute x12 -> x6, starting transfers between devices: 37.2 us -> 10.4 us  [rotate(): return lax.ppermute(value, axis, [(i, (i + step) % 4) for i in range(4)])]
    ppermute x38 -> x21, waiting for transfers between devices: 54.4 us -> 80.6 us  [shift(): return lax.ppermute(value, AXES, pairs)]
    all_gather x0 -> x4, waiting for transfers between devices: none -> 18.6 us  [the longest x2 18.6 us: body(): mixed_parts = [lax.all_gather(mine0, 'tp'), lax.all_gather(mine1, 'tp')]]
    unnamed x104 -> x64, local copies, waits for them, and re-layouts: 3 us -> 15.2 us
    ppermute x0 -> x2, starting transfers between devices: none -> 7.77 us  [transposed(): return lax.ppermute(value, AXES, pairs)]
  transfers between devices with their start and end apart: 50 -> 33, of which waited for: 17 -> 18; matrix products, arithmetic and copies ran while one was open for 5% -> 3% of each run, Pallas kernels for 10% -> 14%
where the time goes in v2:
time: 281 us; the launch traced here: 279 us
  waiting for transfers between devices  144 us (51%)
  starting transfers between devices  51 us (18%)
  Pallas kernels  46.1 us (16%)
  local copies, waits for them, and re-layouts  16.3 us (6%)
  between operations  14.9 us (5%)
  other arithmetic  6.17 us (2%)
    ppermute x21, waiting for transfers between devices, shift(): return lax.ppermute(value, AXES, pairs)  80.6 us
    pallas_call x2, Pallas kernels, attend(): pl.pallas_call(functools.partial(head_kernel, side), out_shape=jax.ShapeD...  34.9 us
    ppermute x21, starting transfers between devices, shift(): return lax.ppermute(value, AXES, pairs)  32.7 us
    ppermute x2, waiting for transfers between devices, transposed(): return lax.ppermute(value, AXES, pairs)  29.4 us
    all_gather x2, waiting for transfers between devices, body(): mixed_parts = [lax.all_gather(mine0, 'tp'), lax.all_gather(mine1, 'tp')]  18.6 us
    ppermute x6, waiting for transfers between devices, rotate(): return lax.ppermute(value, axis, [(i, (i + step) % 4) for i in range(4)])  15.4 us
    unnamed x64, local copies, waits for them, and re-layouts  15.2 us
    ppermute x6, starting transfers between devices, rotate(): return lax.ppermute(value, axis, [(i, (i + step) % 4) for i in range(4)])  10.4 us
  transfers between devices with their start and end apart: 33, of which 18 were waited for; matrix products, arithmetic and copies ran while one was open for 3% of the time, Pallas kernels for 14%

profile of v2, /device:TPU:48, one launch (start us, length us, event | category | flops | bytes accessed | tf_op | source)
XLA Modules:
  0.0 278.5 jit_solution(13926110643131206249)
XLA Ops:
  6.5 0.7 convert_element_type.10
  7.2 1.4 copy.69
  9.4 0.2 copy-done.6
  9.6 0.5 copy.76
  11.0 0.1 copy.93
  11.1 0.1 copy.94
  11.7 0.1 copy.99
  11.9 0.1 copy.100
  12.7 0.6 copy-done.5
  13.4 0.4 collective-permute-start.2
  13.8 2.2 collective-permute-start.3
  16.0 0.2 collective-permute-start.1
  16.2 0.6 dynamic_slice.17
  17.5 4.6 %collective-permute-done.2 = bf16[80,1024]{1,0:T(8,128)(2,1)S(1)} collective-permute-done((bf16[80,1024]{1,0:T(8,128)(2,1)S(1)}, bf16[80,1024]{1,0:T(8,128)(2,1)S(1)}, u32[]{:S(2)}, u32[]{:S(2)}) %collective-permute-start.2) | collective-permute-done | bytes 163872 | tf_op jit(solution)/shard_map/ppermute | solution.py:35
  22.1 1.6 collective-permute-done.3
  23.9 0.7 copy-done.4
  24.6 3.3 %collective-permute-start.11 = (bf16[512,384]{1,0:T(8,128)(2,1)S(1)}, bf16[512,384]{1,0:T(8,128)(2,1)S(1)}, u32[]{:S(2)}, u32[]{:S(2)}) collective-permute-start(bf16[512,384]{1,0:T(8,128)(2,1)S(1)} %get-tuple-element.21), channel_id=1, source_target_pairs={{0,2},{4,6},{1,3},{5,7},{2,8},{6,12},{3,9},{7,13},{8,10},{12,14},{... | collective-permute-start | bytes 1179656 | tf_op jit(solution)/shard_map/ppermute | solution.py:31
  27.9 2.1 collective-permute-start.12
  30.0 16.9 %collective-permute-done.11 = bf16[512,384]{1,0:T(8,128)(2,1)S(1)} collective-permute-done((bf16[512,384]{1,0:T(8,128)(2,1)S(1)}, bf16[512,384]{1,0:T(8,128)(2,1)S(1)}, u32[]{:S(2)}, u32[]{:S(2)}) %collective-permute-start.11) | collective-permute-done | bytes 393248 | tf_op jit(solution)/shard_map/ppermute | solution.py:31
  47.0 1.0 pad_maximum_fusion
  48.0 2.3 collective-permute-start.6
  50.3 3.7 %collective-permute-start.5 = (bf16[80,1024]{1,0:T(8,128)(2,1)S(1)}, bf16[80,1024]{1,0:T(8,128)(2,1)S(1)}, u32[]{:S(2)}, u32[]{:S(2)}) collective-permute-start(bf16[80,1024]{1,0:T(8,128)(2,1)S(1)} %select_select_fusion), channel_id=1, source_target_pairs={{0,2},{1,3},{2,0},{3,1},{4,6},{5,7},{6,4},{7,5},{8,10},{9,11},{10,... | collective-permute-start | bytes 491528 | tf_op jit(solution)/shard_map/ppermute | solution.py:35
  53.9 1.6 collective-permute-start.4
  55.6 8.9 %collective-permute-done.6 = bf16[80,1024]{1,0:T(8,128)(2,1)S(1)} collective-permute-done((bf16[80,1024]{1,0:T(8,128)(2,1)S(1)}, bf16[80,1024]{1,0:T(8,128)(2,1)S(1)}, u32[]{:S(2)}, u32[]{:S(2)}) %collective-permute-start.6) | collective-permute-done | bytes 163872 | tf_op jit(solution)/shard_map/ppermute | solution.py:35
  64.4 0.3 collective-permute-done.4
  65.1 0.7 collective-permute-start.13
  65.8 3.5 %collective-permute-start.14 = (bf16[512,512]{1,0:T(8,128)(2,1)S(1)}, bf16[512,512]{1,0:T(8,128)(2,1)S(1)}, u32[]{:S(2)}, u32[]{:S(2)}) collective-permute-start(bf16[512,512]{1,0:T(8,128)(2,1)S(1)} %fusion.2), channel_id=1, source_target_pairs={{0,10},{4,14},{1,11},{5,15},{2,0},{6,4},{3,1},{7,5},{8,2},{12,6},{... | collective-permute-start | bytes 1572872 | tf_op jit(solution)/shard_map/ppermute | solution.py:31
  69.4 2.8 %collective-permute-start.10 = (bf16[80,1024]{1,0:T(8,128)(2,1)S(1)}, bf16[80,1024]{1,0:T(8,128)(2,1)S(1)}, u32[]{:S(2)}, u32[]{:S(2)}) collective-permute-start(bf16[80,1024]{1,0:T(8,128)(2,1)S(1)} %get-tuple-element.52), channel_id=1, source_target_pairs={{0,48},{4,52},{1,49},{5,53},{2,50},{6,54},{3,51},{7,55},{8,56},{12... | collective-permute-start | bytes 491528 | tf_op jit(solution)/shard_map/ppermute | solution.py:31
  72.2 0.8 collective-permute-start.9
  73.0 7.8 %collective-permute-done.10 = bf16[80,1024]{1,0:T(8,128)(2,1)S(1)} collective-permute-done((bf16[80,1024]{1,0:T(8,128)(2,1)S(1)}, bf16[80,1024]{1,0:T(8,128)(2,1)S(1)}, u32[]{:S(2)}, u32[]{:S(2)}) %collective-permute-start.10) | collective-permute-done | bytes 163872 | tf_op jit(solution)/shard_map/ppermute | solution.py:31
  80.8 0.3 collective-permute-start.8
  81.1 2.6 collective-permute-done.9
  83.8 9.1 %collective-permute-done.8 = bf16[80,1024]{1,0:T(8,128)(2,1)S(1)} collective-permute-done((bf16[80,1024]{1,0:T(8,128)(2,1)S(1)}, bf16[80,1024]{1,0:T(8,128)(2,1)S(1)}, u32[]{:S(2)}, u32[]{:S(2)}) %collective-permute-start.8) | collective-permute-done | bytes 163872 | tf_op jit(solution)/shard_map/ppermute | solution.py:31
  93.0 2.1 collective-permute-done.15.text_other
  95.1 2.6 collective-permute-start.19
  97.7 1.6 collective-permute-start.20
  99.3 11.2 %collective-permute-done.19 = bf16[512,384]{1,0:T(8,128)(2,1)S(1)} collective-permute-done((bf16[512,384]{1,0:T(8,128)(2,1)S(1)}, bf16[512,384]{1,0:T(8,128)(2,1)S(1)}, u32[]{:S(2)}, u32[]{:S(2)}) %collective-permute-start.19) | collective-permute-done | bytes 393248 | tf_op jit(solution)/shard_map/ppermute | solution.py:31
  110.4 0.8 collective-permute-done.20
  111.2 1.0 pad_maximum_fusion.1
  112.6 3.3 %shard_map.73 = (f32[160,512]{1,0:T(8,128)S(1)}, bf16[160,512]{1,0:T(8,128)(2,1)S(1)}, bf16[160,512]{1,0:T(8,128)(2,1)S(1)}, bf16[160,512]{1,0:T(8,128)(2,1)S(1)}) custom-call(s32[4]{0:T(128)S(1)} %and_select_fusion.table, bf16[4,80,1024]{2,1,0:T(8,128)(2,1)S(1)} %pad_maximum_fusion.3.text_own, bf16[4,80,1024]{2,1,0:T(8,128)(2,1)S(1)} %collective-permute-done.15.text_other, ...), custom_call_target="tpu_custom_call" | custom-call | flops 671088640 | bytes 4194304 | tf_op jit(solution)/shard_map/pallas_call | solution.py:92
  115.9 7.3 %collective-permute-start.16 = (bf16[160,512]{1,0:T(8,128)(2,1)S(1)}, bf16[160,512]{1,0:T(8,128)(2,1)S(1)}, u32[]{:S(2)}, u32[]{:S(2)}) collective-permute-start(bf16[160,512]{1,0:T(8,128)(2,1)S(1)} %get-tuple-element.25), channel_id=1, source_target_pairs={{0,16},{4,20},{1,17},{5,21},{2,18},{6,22},{3,19},{7,23},{8,24},{12... | collective-permute-start | bytes 491528 | tf_op jit(solution)/shard_map/ppermute | solution.py:31
  123.2 1.3 collective-permute-start.17
  124.5 2.5 collective-permute-start.18
  127.0 0.7 slice_convert_fusion
  127.8 4.0 %collective-permute-done.17.rest_2_ = bf16[160,512]{1,0:T(8,128)(2,1)S(1)} collective-permute-done((bf16[160,512]{1,0:T(8,128)(2,1)S(1)}, bf16[160,512]{1,0:T(8,128)(2,1)S(1)}, u32[]{:S(2)}, u32[]{:S(2)}) %collective-permute-start.17) | collective-permute-done | bytes 163872 | tf_op jit(solution)/shard_map/ppermute | solution.py:31
  131.8 2.1 copy-done
  134.0 17.4 %shard_map.74 = bf16[6,256,128]{2,1,0:T(8,128)(2,1)S(1)} custom-call(s32[16]{0:T(128)S(1)} %stack.327.table, s32[2,3]{1,0:T(2,128)S(1)} %pad_add_fusion.lengths, bf16[768,4096]{1,0:T(8,128)(2,1)} %bitcast.150, bf16[768,4096]{1,0:T(8,128)(2,1)} %collective-permute-done.7.image_other, f32[160,512]{1,0:T(8,128)S(1)} %get-tuple-element.24.rest_0_, ...), custom_call_target="tpu_custom_call" | custom-call | flops 6442450944 | bytes 16777216 | tf_op jit(solution)/shard_map/pallas_call | solution.py:191
  151.6 1.4 collective-permute-done.21
  153.0 0.8 pad_maximum_fusion.5
  153.9 7.2 %collective-permute-start.22 = (bf16[512,256]{1,0:T(8,128)(2,1)S(1)}, bf16[512,256]{1,0:T(8,128)(2,1)S(1)}, u32[]{:S(2)}, u32[]{:S(2)}) collective-permute-start(bf16[512,256]{1,0:T(8,128)(2,1)S(1)} %bitcast.152), channel_id=1, source_target_pairs={{0,0},{4,4},{1,16},{5,20},{2,32},{6,36},{3,48},{7,52},{8,8},{12,12... | collective-permute-start | bytes 786440 | tf_op jit(solution)/shard_map/ppermute | solution.py:49
  161.1 0.5 collective-permute-start.23
  161.6 29.4 %collective-permute-done.22 = bf16[512,256]{1,0:T(8,128)(2,1)S(1)} collective-permute-done((bf16[512,256]{1,0:T(8,128)(2,1)S(1)}, bf16[512,256]{1,0:T(8,128)(2,1)S(1)}, u32[]{:S(2)}, u32[]{:S(2)}) %collective-permute-start.22) | collective-permute-done | bytes 262176 | tf_op jit(solution)/shard_map/ppermute | solution.py:49
  191.2 1.9 copy-done.1
  193.1 17.4 %shard_map.75 = bf16[6,256,128]{2,1,0:T(8,128)(2,1)S(1)} custom-call(s32[16]{0:T(128)S(1)} %stack.327.table, s32[2,3]{1,0:T(2,128)S(1)} %pad_add_fusion.lengths, bf16[768,4096]{1,0:T(8,128)(2,1)} %bitcast.151, bf16[768,4096]{1,0:T(8,128)(2,1)} %collective-permute-done.7.image_other, f32[160,512]{1,0:T(8,128)S(1)} %get-tuple-element.24.rest_0_, ...), custom_call_target="tpu_custom_call" | custom-call | flops 6442450944 | bytes 16777216 | tf_op jit(solution)/shard_map/pallas_call | solution.py:191
  210.6 1.4 collective-permute-done.24
  212.1 0.8 pad_maximum_fusion.6
  212.9 3.2 %collective-permute-start.26 = (bf16[1024,256]{1,0:T(8,128)(2,1)S(1)}, bf16[1024,256]{1,0:T(8,128)(2,1)}, u32[]{:S(2)}, u32[]{:S(2)}) collective-permute-start(bf16[1024,256]{1,0:T(8,128)(2,1)S(1)} %constant_dynamic-update-slice_fusion), channel_id=1, source_target_pairs={{0,48},{4,52},{1,49},{5,53},{2,50},{6,54},{3,51},{7,55},{8,56},{12... | collective-permute-start | bytes 1572872 | tf_op jit(solution)/shard_map/ppermute | solution.py:31
  216.2 23.2 %collective-permute-done.25 = bf16[1024,256]{1,0:T(8,128)(2,1)} collective-permute-done((bf16[1024,256]{1,0:T(8,128)(2,1)S(1)}, bf16[1024,256]{1,0:T(8,128)(2,1)}, u32[]{:S(2)}, u32[]{:S(2)}) %collective-permute-start.25) | collective-permute-done | bytes 524320 | tf_op jit(solution)/shard_map/ppermute | solution.py:31
  239.4 1.1 constant_dynamic-update-slice_fusion.4
  240.5 1.1 constant_dynamic-update-slice_fusion.3
  242.6 18.6 %all-gather.15.cloned.1.call-done = bf16[3072,256]{1,0:T(8,128)(2,1)} async-done(((bf16[768,256]{1,0:T(8,128)(2,1)}), bf16[3072,256]{1,0:T(8,128)(2,1)}) %all-gather.15.cloned.1.call-update) | async-done | bytes 1572880 | tf_op jit(solution)/shard_map/all_gather | solution.py:340
  261.2 1.4 copy-done.2
  262.6 1.4 copy-done.3
  264.0 7.9 %shard_map.76 = bf16[768,1024]{1,0:T(8,128)(2,1)} custom-call(s32[16,2]{1,0:T(8,128)S(1)} %stack.307.spots, s32[2]{0:T(128)S(1)} %pad_add_fusion.1.heads, bf16[4,768,256]{2,1,0:T(8,128)(2,1)S(1)} %bitcast.132, bf16[4,768,256]{2,1,0:T(8,128)(2,1)S(1)} %bitcast.133, bf16[4096,256]{1,0:T(8,128)(2,1)S(1)} %constant_dynamic-update-slice_fusion.2.rest_2_, ...), custom_call_target="tpu_custom_call" | custom-call | flops 3221225472 | bytes 9437184 | tf_op jit(solution)/shard_map/pallas_call | solution.py:250
  (111 shorter events, 4.9 us)
Async XLA Ops:
  6.5 125.3 %all-gather.9.cloned.1.call-start = ((), (), s32[]{:S(2)}) async-start(), calls=%async_computation | async-start | bytes 3932160 | tf_op jit(solution)/shard_map/all_gather | solution.py:58
  8.6 1.0 copy-start.6
  12.5 0.9 copy-start.5
  12.5 3.8 %copy-start.9 = (s32[4]{0:T(128)S(1)}, s32[4]{0:T(128)}, u32[]{:S(2)}) copy-start(s32[4]{0:T(128)} %param.10) | copy-start | bytes 52
  12.6 11.1 %collective-permute-start = (bf16[272,1280]{1,0:T(8,128)(2,1)S(1)}, bf16[272,1280]{1,0:T(8,128)(2,1)S(1)}, u32[]{:S(2)}, u32[]{:S(2)}) collective-permute-start(bf16[272,1280]{1,0:T(8,128)(2,1)S(1)} %fusion.1), channel_id=1, source_target_pairs={{0,4},{4,0},{1,5},{5,1},{2,6},{6,2},{3,7},{7,3},{8,12},{12,8},{9,1... | collective-permute-start | bytes 2088968 | tf_op jit(solution)/shard_map/ppermute | solution.py:31
  13.4 8.7 %collective-permute-start.2 = (bf16[80,1024]{1,0:T(8,128)(2,1)S(1)}, bf16[80,1024]{1,0:T(8,128)(2,1)S(1)}, u32[]{:S(2)}, u32[]{:S(2)}) collective-permute-start(bf16[80,1024]{1,0:T(8,128)(2,1)S(1)} %pad.9), channel_id=1, source_target_pairs={{0,128},{64,192},{128,0},{192,64},{1,129},{65,193},{129,1},{193,65... | collective-permute-start | bytes 491528 | tf_op jit(solution)/shard_map/ppermute | solution.py:35
  13.8 9.9 %collective-permute-start.3 = (bf16[80,1024]{1,0:T(8,128)(2,1)S(1)}, bf16[80,1024]{1,0:T(8,128)(2,1)S(1)}, u32[]{:S(2)}, u32[]{:S(2)}) collective-permute-start(bf16[80,1024]{1,0:T(8,128)(2,1)S(1)} %pad.9), channel_id=1, source_target_pairs={{0,64},{64,128},{128,192},{192,0},{1,65},{65,129},{129,193},{193,1... | collective-permute-start | bytes 491528 | tf_op jit(solution)/shard_map/ppermute | solution.py:35
  16.0 7.7 %collective-permute-start.1 = (bf16[80,1024]{1,0:T(8,128)(2,1)S(1)}, bf16[80,1024]{1,0:T(8,128)(2,1)S(1)}, u32[]{:S(2)}, u32[]{:S(2)}) collective-permute-start(bf16[80,1024]{1,0:T(8,128)(2,1)S(1)} %pad.9), channel_id=1, source_target_pairs={{0,192},{64,0},{128,64},{192,128},{1,193},{65,1},{129,65},{193,129... | collective-permute-start | bytes 491528 | tf_op jit(solution)/shard_map/ppermute | solution.py:35
  23.8 0.9 copy-start.4
  24.6 22.3 %collective-permute-start.11 = (bf16[512,384]{1,0:T(8,128)(2,1)S(1)}, bf16[512,384]{1,0:T(8,128)(2,1)S(1)}, u32[]{:S(2)}, u32[]{:S(2)}) collective-permute-start(bf16[512,384]{1,0:T(8,128)(2,1)S(1)} %get-tuple-element.21), channel_id=1, source_target_pairs={{0,2},{4,6},{1,3},{5,7},{2,8},{6,12},{3,9},{7,13},{8,10},{12,14},{... | collective-permute-start | bytes 1179656 | tf_op jit(solution)/shard_map/ppermute | solution.py:31
  27.9 19.1 %collective-permute-start.12 = (bf16[512,384]{1,0:T(8,128)(2,1)S(1)}, bf16[512,384]{1,0:T(8,128)(2,1)S(1)}, u32[]{:S(2)}, u32[]{:S(2)}) collective-permute-start(bf16[512,384]{1,0:T(8,128)(2,1)S(1)} %get-tuple-element.21), channel_id=1, source_target_pairs={{0,10},{4,14},{1,11},{5,15},{2,0},{6,4},{3,1},{7,5},{8,2},{12,6},{... | collective-permute-start | bytes 1179656 | tf_op jit(solution)/shard_map/ppermute | solution.py:31
  48.0 143.2 %all-gather.13.cloned.1.call-start = ((), (), s32[]{:S(2)}) async-start(), calls=%async_computation.2 | async-start | bytes 3932160 | tf_op jit(solution)/shard_map/all_gather | solution.py:58
  48.0 16.4 %collective-permute-start.6 = (bf16[80,1024]{1,0:T(8,128)(2,1)S(1)}, bf16[80,1024]{1,0:T(8,128)(2,1)S(1)}, u32[]{:S(2)}, u32[]{:S(2)}) collective-permute-start(bf16[80,1024]{1,0:T(8,128)(2,1)S(1)} %select_select_fusion), channel_id=1, source_target_pairs={{0,3},{1,0},{2,1},{3,2},{4,7},{5,4},{6,5},{7,6},{8,11},{9,8},{10,9... | collective-permute-start | bytes 491528 | tf_op jit(solution)/shard_map/ppermute | solution.py:35
  50.3 14.2 %collective-permute-start.5 = (bf16[80,1024]{1,0:T(8,128)(2,1)S(1)}, bf16[80,1024]{1,0:T(8,128)(2,1)S(1)}, u32[]{:S(2)}, u32[]{:S(2)}) collective-permute-start(bf16[80,1024]{1,0:T(8,128)(2,1)S(1)} %select_select_fusion), channel_id=1, source_target_pairs={{0,2},{1,3},{2,0},{3,1},{4,6},{5,7},{6,4},{7,5},{8,10},{9,11},{10,... | collective-permute-start | bytes 491528 | tf_op jit(solution)/shard_map/ppermute | solution.py:35
  53.9 10.8 %collective-permute-start.4 = (bf16[80,1024]{1,0:T(8,128)(2,1)S(1)}, bf16[80,1024]{1,0:T(8,128)(2,1)S(1)}, u32[]{:S(2)}, u32[]{:S(2)}) collective-permute-start(bf16[80,1024]{1,0:T(8,128)(2,1)S(1)} %select_select_fusion), channel_id=1, source_target_pairs={{0,1},{1,2},{2,3},{3,0},{4,5},{5,6},{6,7},{7,4},{8,9},{9,10},{10,1... | collective-permute-start | bytes 491528 | tf_op jit(solution)/shard_map/ppermute | solution.py:35
  64.8 67.0 %collective-permute-start.7 = (bf16[768,4096]{1,0:T(8,128)(2,1)}, bf16[768,4096]{1,0:T(8,128)(2,1)}, u32[]{:S(2)}, u32[]{:S(2)}) collective-permute-start(bf16[768,4096]{1,0:T(8,128)(2,1)} %bitcast.149), channel_id=1, source_target_pairs={{0,4},{4,0},{1,5},{5,1},{2,6},{6,2},{3,7},{7,3},{8,12},{12,8},{9,1... | collective-permute-start | bytes 18874376 | tf_op jit(solution)/shard_map/ppermute | solution.py:31
  65.1 27.9 %collective-permute-start.13 = (bf16[512,512]{1,0:T(8,128)(2,1)S(1)}, bf16[512,512]{1,0:T(8,128)(2,1)S(1)}, u32[]{:S(2)}, u32[]{:S(2)}) collective-permute-start(bf16[512,512]{1,0:T(8,128)(2,1)S(1)} %fusion.2), channel_id=1, source_target_pairs={{0,2},{4,6},{1,3},{5,7},{2,8},{6,12},{3,9},{7,13},{8,10},{12,14},{... | collective-permute-start | bytes 1572872 | tf_op jit(solution)/shard_map/ppermute | solution.py:31
  65.8 27.1 %collective-permute-start.14 = (bf16[512,512]{1,0:T(8,128)(2,1)S(1)}, bf16[512,512]{1,0:T(8,128)(2,1)S(1)}, u32[]{:S(2)}, u32[]{:S(2)}) collective-permute-start(bf16[512,512]{1,0:T(8,128)(2,1)S(1)} %fusion.2), channel_id=1, source_target_pairs={{0,10},{4,14},{1,11},{5,15},{2,0},{6,4},{3,1},{7,5},{8,2},{12,6},{... | collective-permute-start | bytes 1572872 | tf_op jit(solution)/shard_map/ppermute | solution.py:31
  69.4 11.5 %collective-permute-start.10 = (bf16[80,1024]{1,0:T(8,128)(2,1)S(1)}, bf16[80,1024]{1,0:T(8,128)(2,1)S(1)}, u32[]{:S(2)}, u32[]{:S(2)}) collective-permute-start(bf16[80,1024]{1,0:T(8,128)(2,1)S(1)} %get-tuple-element.52), channel_id=1, source_target_pairs={{0,48},{4,52},{1,49},{5,53},{2,50},{6,54},{3,51},{7,55},{8,56},{12... | collective-permute-start | bytes 491528 | tf_op jit(solution)/shard_map/ppermute | solution.py:31
  72.2 11.6 %collective-permute-start.9 = (bf16[80,1024]{1,0:T(8,128)(2,1)S(1)}, bf16[80,1024]{1,0:T(8,128)(2,1)S(1)}, u32[]{:S(2)}, u32[]{:S(2)}) collective-permute-start(bf16[80,1024]{1,0:T(8,128)(2,1)S(1)} %get-tuple-element.53), channel_id=1, source_target_pairs={{0,32},{4,36},{1,33},{5,37},{2,34},{6,38},{3,35},{7,39},{8,40},{12... | collective-permute-start | bytes 491528 | tf_op jit(solution)/shard_map/ppermute | solution.py:31
  80.8 12.0 %collective-permute-start.8 = (bf16[80,1024]{1,0:T(8,128)(2,1)S(1)}, bf16[80,1024]{1,0:T(8,128)(2,1)S(1)}, u32[]{:S(2)}, u32[]{:S(2)}) collective-permute-start(bf16[80,1024]{1,0:T(8,128)(2,1)S(1)} %get-tuple-element.54), channel_id=1, source_target_pairs={{0,16},{4,20},{1,17},{5,21},{2,18},{6,22},{3,19},{7,23},{8,24},{12... | collective-permute-start | bytes 491528 | tf_op jit(solution)/shard_map/ppermute | solution.py:31
  92.9 2.2 collective-permute-start.15
  95.1 15.3 %collective-permute-start.19 = (bf16[512,384]{1,0:T(8,128)(2,1)S(1)}, bf16[512,384]{1,0:T(8,128)(2,1)S(1)}, u32[]{:S(2)}, u32[]{:S(2)}) collective-permute-start(bf16[512,384]{1,0:T(8,128)(2,1)S(1)} %get-tuple-element.28), channel_id=1, source_target_pairs={{0,2},{4,6},{1,3},{5,7},{2,8},{6,12},{3,9},{7,13},{8,10},{12,14},{... | collective-permute-start | bytes 1179656 | tf_op jit(solution)/shard_map/ppermute | solution.py:31
  97.7 13.5 %collective-permute-start.20 = (bf16[512,384]{1,0:T(8,128)(2,1)S(1)}, bf16[512,384]{1,0:T(8,128)(2,1)S(1)}, u32[]{:S(2)}, u32[]{:S(2)}) collective-permute-start(bf16[512,384]{1,0:T(8,128)(2,1)S(1)} %get-tuple-element.28), channel_id=1, source_target_pairs={{0,10},{4,14},{1,11},{5,15},{2,0},{6,4},{3,1},{7,5},{8,2},{12,6},{... | collective-permute-start | bytes 1179656 | tf_op jit(solution)/shard_map/ppermute | solution.py:31
  112.2 15.5 %copy-start.7 = (s32[1,3]{1,0:T(1,128)S(1)}, s32[1,3]{1,0:T(1,128)}, u32[]{:S(2)}) copy-start(s32[1,3]{1,0:T(1,128)} %param.9) | copy-start | bytes 40
  112.2 130.4 %all-gather.11.cloned.1.call-start = ((), (), s32[]{:S(2)}) async-start(), calls=%async_computation.1 | async-start | bytes 1966080 | tf_op jit(solution)/shard_map/all_gather | solution.py:340
  115.9 11.9 %collective-permute-start.16 = (bf16[160,512]{1,0:T(8,128)(2,1)S(1)}, bf16[160,512]{1,0:T(8,128)(2,1)S(1)}, u32[]{:S(2)}, u32[]{:S(2)}) collective-permute-start(bf16[160,512]{1,0:T(8,128)(2,1)S(1)} %get-tuple-element.25), channel_id=1, source_target_pairs={{0,16},{4,20},{1,17},{5,21},{2,18},{6,22},{3,19},{7,23},{8,24},{12... | collective-permute-start | bytes 491528 | tf_op jit(solution)/shard_map/ppermute | solution.py:31
  123.2 8.7 %collective-permute-start.17 = (bf16[160,512]{1,0:T(8,128)(2,1)S(1)}, bf16[160,512]{1,0:T(8,128)(2,1)S(1)}, u32[]{:S(2)}, u32[]{:S(2)}) collective-permute-start(bf16[160,512]{1,0:T(8,128)(2,1)S(1)} %get-tuple-element.26), channel_id=1, source_target_pairs={{0,32},{4,36},{1,33},{5,37},{2,34},{6,38},{3,35},{7,39},{8,40},{12... | collective-permute-start | bytes 491528 | tf_op jit(solution)/shard_map/ppermute | solution.py:31
  124.5 7.3 %collective-permute-start.18 = (bf16[160,512]{1,0:T(8,128)(2,1)S(1)}, bf16[160,512]{1,0:T(8,128)(2,1)S(1)}, u32[]{:S(2)}, u32[]{:S(2)}) collective-permute-start(bf16[160,512]{1,0:T(8,128)(2,1)S(1)} %get-tuple-element.27), channel_id=1, source_target_pairs={{0,48},{4,52},{1,49},{5,53},{2,50},{6,54},{3,51},{7,55},{8,56},{12... | collective-permute-start | bytes 491528 | tf_op jit(solution)/shard_map/ppermute | solution.py:31
  131.8 2.1 copy-start
  151.4 2.4 copy-start.8
  151.5 1.5 collective-permute-start.21
  153.8 107.4 %all-gather.15.cloned.1.call-start = ((), (), s32[]{:S(2)}) async-start(), calls=%async_computation.3 | async-start | bytes 1966080 | tf_op jit(solution)/shard_map/all_gather | solution.py:340
  153.9 37.2 %collective-permute-start.22 = (bf16[512,256]{1,0:T(8,128)(2,1)S(1)}, bf16[512,256]{1,0:T(8,128)(2,1)S(1)}, u32[]{:S(2)}, u32[]{:S(2)}) collective-permute-start(bf16[512,256]{1,0:T(8,128)(2,1)S(1)} %bitcast.152), channel_id=1, source_target_pairs={{0,0},{4,4},{1,16},{5,20},{2,32},{6,36},{3,48},{7,52},{8,8},{12,12... | collective-permute-start | bytes 786440 | tf_op jit(solution)/shard_map/ppermute | solution.py:49
  161.1 30.0 %collective-permute-start.23 = (bf16[512,256]{1,0:T(8,128)(2,1)S(1)}, bf16[512,256]{1,0:T(8,128)(2,1)S(1)}, u32[]{:S(2)}, u32[]{:S(2)}) collective-permute-start(bf16[512,256]{1,0:T(8,128)(2,1)S(1)} %bitcast.153), channel_id=1, source_target_pairs={{0,8},{4,12},{1,24},{5,28},{2,40},{6,44},{3,56},{7,60},{8,0},{12,4... | collective-permute-start | bytes 786440 | tf_op jit(solution)/shard_map/ppermute | solution.py:49
  191.2 1.9 copy-start.1
  210.5 1.5 collective-permute-start.24
  212.9 26.5 %collective-permute-start.25 = (bf16[1024,256]{1,0:T(8,128)(2,1)S(1)}, bf16[1024,256]{1,0:T(8,128)(2,1)}, u32[]{:S(2)}, u32[]{:S(2)}) collective-permute-start(bf16[1024,256]{1,0:T(8,128)(2,1)S(1)} %constant_dynamic-update-slice_fusion), channel_id=1, source_target_pairs={{0,16},{4,20},{1,17},{5,21},{2,18},{6,22},{3,19},{7,23},{8,24},{12... | collective-permute-start | bytes 1572872 | tf_op jit(solution)/shard_map/ppermute | solution.py:31
  212.9 27.6 %collective-permute-start.26 = (bf16[1024,256]{1,0:T(8,128)(2,1)S(1)}, bf16[1024,256]{1,0:T(8,128)(2,1)}, u32[]{:S(2)}, u32[]{:S(2)}) collective-permute-start(bf16[1024,256]{1,0:T(8,128)(2,1)S(1)} %constant_dynamic-update-slice_fusion), channel_id=1, source_target_pairs={{0,48},{4,52},{1,49},{5,53},{2,50},{6,54},{3,51},{7,55},{8,56},{12... | collective-permute-start | bytes 1572872 | tf_op jit(solution)/shard_map/ppermute | solution.py:31
  216.1 25.5 %collective-permute-start.27 = (bf16[1024,256]{1,0:T(8,128)(2,1)S(1)}, bf16[1024,256]{1,0:T(8,128)(2,1)S(1)}, u32[]{:S(2)}, u32[]{:S(2)}) collective-permute-start(bf16[1024,256]{1,0:T(8,128)(2,1)S(1)} %constant_dynamic-update-slice_fusion), channel_id=1, source_target_pairs={{0,32},{4,36},{1,33},{5,37},{2,34},{6,38},{3,35},{7,39},{8,40},{12... | collective-permute-start | bytes 1572872 | tf_op jit(solution)/shard_map/ppermute | solution.py:31
  241.6 19.6 %collective-permute-start.28 = (bf16[4096,256]{1,0:T(8,128)(2,1)S(1)}, bf16[4096,256]{1,0:T(8,128)(2,1)}, u32[]{:S(2)}, u32[]{:S(2)}) collective-permute-start(bf16[4096,256]{1,0:T(8,128)(2,1)S(1)} %constant_dynamic-update-slice_fusion.2.rest_2_), channel_id=1, source_target_pairs={{0,4},{4,0},{1,5},{5,1},{2,6},{6,2},{3,7},{7,3},{8,12},{12,8},{9,1... | collective-permute-start | bytes 6291464 | tf_op jit(solution)/shard_map/ppermute | solution.py:31
  261.2 1.4 copy-start.2
  262.6 1.4 copy-start.3
Sparse Core Ops, SparseCore 0:
  48.1 50.9 all-gather.8
  112.3 48.4 all-gather.12
  162.6 46.8 all-gather.10
  216.3 44.9 all-gather.14
